TPU v7x, 32 devices: a whole 2x2x4 slice. The times are simulated.
32 devices in a mesh: orb: 32 (over z, y, x, core).
Axes of the slice: x: 2, y: 2, z: 4, core: 2. Of those that a mesh axis runs over, the one named last changes fastest.
Arguments:
- slabs: float32 [64, 384, 768], P('orb'), may hold values from -1.2 to 1.2
- amplitudes: float32 [256, 384, 384], P('orb'), may hold values from -6 to 6
- intersections: float32 [256, 3, 384, 384], P('orb'), may hold values from -0.3125 to 0.3125
- fock_coupling: float32 [256, 3], P('orb'), may hold values from -0.9 to 0.9
- virt_energy: float32 [256, 384], P('orb'), may hold values from 0.4 to 4
- occ_pair_energy: float32 [256], P('orb'), may hold values from -2.4 to -0.4
- pair_orbs: int32 [256, 2], P('orb'), may hold values from 0 to 63, as said below
- couplings: int32 [256, 3], P('orb'), may hold values from 0 to 255, as said below
Outputs:
- updated_amplitudes: float32 [256, 384, 384], P('orb')
Inputs may be any that keep to these rules, and one draw needn't show every extreme that they name: `pair_orbs`: row p holds orbitals (i, j), i != j. A device's block of 8 rows has i among that device's own 2 orbitals (rows of its block of slabs) and j among the orbitals of a device at most 2 away along the axis, counted without wrapping (the first and last devices are not neighbours here); every device's block names orbitals of some device 2 away and of some device next to it. `couplings`: entry (p, c) is a pair coupled to pair p. For c = 0 it is a pair in the block of the device before p's owner, and for c = 1 a pair in the block of the device after it. The axis closes: before the first device comes the last one, and after the last comes the first. Over one device's block of 8 rows, column 0 names exactly 4 distinct pairs, and so does column 1. For c = 2 it is another pair of p's own block.
All inputs are finite; a program needn't handle non-finite values.
Results may differ from a plain program's by a relative error of at most 0.0001.
Values sent between devices are 32-bit elements; how exact they have to be, the bound alone decides.
No kernel may reach another device: no remote copies, remote signals or barrier semaphores. Data moves between devices by JAX's collectives and lax.ppermute only.
A program may use at most 192 MiB of HBM per device.

v0:
```python
import jax
import jax.numpy as jnp
from jax import lax
from jax.sharding import PartitionSpec as P

REACH = 2
ITERS = 2


highest = lax.Precision.HIGHEST


def shifted(value, axis, by):
    peers = lax.axis_size(axis)
    pairs = [(i, i + by) for i in range(peers) if 0 <= i + by < peers]
    return lax.ppermute(value, axis, pairs)


def with_halo(cells, sides, width):
    for axis, dim in sides:
        count = lax.axis_size(axis)
        head = lax.slice_in_dim(cells, 0, width, axis=dim)
        tail = lax.slice_in_dim(cells, cells.shape[dim] - width, cells.shape[dim], axis=dim)
        cells = jnp.concatenate(
            [
                lax.ppermute(tail, axis, [(i, (i + 1) % count) for i in range(count)]),
                cells,
                lax.ppermute(head, axis, [((i + 1) % count, i) for i in range(count)]),
            ],
            axis=dim,
        )
    return cells


def fetch_window(slabs):
    pieces = {0: slabs}
    for distance in range(1, REACH + 1):
        for sign in (1, -1):
            pieces[sign * distance] = shifted(slabs, "orb", sign * distance)
    return jnp.concatenate([pieces[-offset] for offset in range(-REACH, REACH + 1)], axis=0)


def distinct_rows(values, count):
    return jnp.unique(values, size=count, fill_value=0).astype(jnp.int32)


def rank_in(sorted_rows, values):
    return jnp.sum((sorted_rows[None, :] < values[:, None]).astype(jnp.int32), axis=1)


def shards(
    slabs,
    amplitudes,
    intersections,
    fock_coupling,
    virt_energy,
    occ_pair_energy,
    pair_orbs,
    couplings,
):
    device = lax.axis_index("orb")
    orbitals_here = slabs.shape[0]
    pairs_here = amplitudes.shape[0]
    half_count = pairs_here // 2
    window = fetch_window(slabs)
    local_first = pair_orbs[:, 0] - device * orbitals_here
    window_second = pair_orbs[:, 1] - (device - REACH) * orbitals_here
    left = jnp.take(slabs, local_first, axis=0)
    right = jnp.take(window, window_second, axis=0)
    integrals = jnp.einsum(
        "paq,pbq->pab", left, right, precision=highest, preferred_element_type=jnp.float32
    )
    denominator = virt_energy[:, :, None] + virt_energy[:, None, :] - occ_pair_energy[:, None, None]
    own_index = pairs_here + couplings[:, 2] - device * pairs_here
    neighbour_lists = with_halo(couplings, (("orb", 0),), pairs_here)
    for_down = distinct_rows(neighbour_lists[:pairs_here, 1], half_count) - device * pairs_here
    for_up = distinct_rows(neighbour_lists[2 * pairs_here :, 0], half_count) - device * pairs_here
    wanted_lower = distinct_rows(couplings[:, 0], half_count)
    wanted_upper = distinct_rows(couplings[:, 1], half_count)
    lower_index = rank_in(wanted_lower, couplings[:, 0])
    upper_index = half_count + pairs_here + rank_in(wanted_upper, couplings[:, 1])
    own_index = own_index - pairs_here + half_count
    coupled_index = jnp.stack([lower_index, upper_index, own_index], axis=1)
    current = amplitudes
    for step in range(ITERS):
        outgoing = jnp.concatenate(
            [jnp.take(current, for_down, axis=0), jnp.take(current, for_up, axis=0)], axis=0
        )
        received = with_halo(outgoing, (("orb", 0),), half_count)
        nearby = jnp.concatenate(
            [received[:half_count], current, received[half_count + pairs_here :]], axis=0
        )

        def project_pair(row):
            chosen_rows, gains, intersection = row
            picked = jnp.take(nearby, chosen_rows, axis=0)
            half = jnp.einsum(
                "cab,cbe->cae",
                intersection,
                picked,
                precision=highest,
                preferred_element_type=jnp.float32,
            )
            whole = jnp.einsum(
                "cae,cfe->caf",
                half,
                intersection,
                precision=highest,
                preferred_element_type=jnp.float32,
            )
            return jnp.sum(gains[:, None, None] * whole, axis=0)

        coupled = lax.map(project_pair, (coupled_index, fock_coupling, intersections))
        residual = integrals + denominator * current - coupled
        current = current - residual / denominator
    return current


def solution(mesh):
    in_specs = (
        P("orb", None, None),
        P("orb", None, None),
        P("orb", None, None, None),
        P("orb", None),
        P("orb", None),
        P("orb"),
        P("orb", None),
        P("orb", None),
    )
    out_specs = P("orb", None, None)
    return jax.shard_map(shards, mesh=mesh, in_specs=in_specs, out_specs=out_specs, check_vma=False)
```

profile of v0, /device:TPU:1, one launch (start us, length us, event | category | flops | bytes accessed | tf_op | source)
XLA Modules:
  0.0 574.9 jit_solution(13296730067184972255)
XLA Ops:
  2.6 4.6 collective-permute-start
  42.2 4.6 gather_fusion.11
  50.1 105.9 %collective-permute-done = f32[2,384,768]{2,1,0:T(8,128)} collective-permute-done((f32[2,384,768]{2,1,0:T(8,128)}, f32[2,384,768]{2,1,0:T(8,128)}, u32[]{:S(2)}, u32[]{:S(2)}) %collective-permute-start) | collective-permute-done | bytes 2359328 | tf_op jit(solution)/shard_map/ppermute | solution.py:16
  156.0 6.9 %collective-permute-start.5 = (f32[4,384,384]{2,1,0:T(8,128)}, f32[4,384,384]{2,1,0:T(8,128)}, u32[]{:S(2)}, u32[]{:S(2)}) collective-permute-start(f32[4,384,384]{2,1,0:T(8,128)} %broadcast_select_fusion.3), channel_id=1, source_target_pairs={{0,1},{1,2},{2,3},{3,4},{4,5},{5,6},{6,7},{7,8},{8,9},{9,10},{10,1... | collective-permute-start | bytes 7077896 | tf_op jit(solution)/shard_map/ppermute | solution.py:26
  163.2 4.7 gather_fusion.2
  171.0 12.5 %collective-permute-done.1 = f32[2,384,768]{2,1,0:T(8,128)} collective-permute-done((f32[2,384,768]{2,1,0:T(8,128)}, f32[2,384,768]{2,1,0:T(8,128)}, u32[]{:S(2)}, u32[]{:S(2)}) %collective-permute-start.1) | collective-permute-done | bytes 2359328 | tf_op jit(solution)/shard_map/ppermute | solution.py:16
  194.8 9.2 %gather_fusion.3 = f32[8,384,768]{2,1,0:T(8,128)} fusion(f32[10,384,768]{2,1,0:T(8,128)} %constant_dynamic-update-slice_fusion, s32[1024]{0:T(1024)S(1)} %get-tuple-element.190), kind=kCustom, calls=%fused_computation.11 | custom fusion | bytes 18874400 | tf_op jit(solution)/shard_map/jit(_take)/gather | solution.py:69
  204.0 19.6 %fusion.32 = f32[8,384,384]{2,1,0:T(8,128)} fusion(f32[8,384,768]{2,1,0:T(8,128)} %gather_fusion.3, f32[8,384,768]{2,1,0:T(8,128)} %gather_fusion.2, pred[8]{0:T(512)(128)(4,1)S(1)} %get-tuple-element.184, pred[8]{0:T(512)(128)(4,1)S(1)} %get-tuple-element.173), kind=kOutput, calls=%fused_computation.64 | convolution fusion | flops 10876354560 | bytes 23592976 | tf_op jit(solution)/shard_map/paq,pbq->pab/dot_general | solution.py:70
  223.6 8.3 %pad_maximum_fusion = f32[16,384,384]{2,1,0:T(8,128)} fusion(f32[4,384,384]{2,1,0:T(8,128)} %collective-permute-done.7, f32[8,384,384]{2,1,0:T(8,128)} %param.20, f32[4,384,384]{2,1,0:T(8,128)} %collective-permute-done.5), kind=kLoop, calls=%fused_computation.62 | loop fusion | flops 4718592 | bytes 18874368 | tf_op jit(solution)/shard_map/concatenate | solution.py:90
  234.4 125.3 %while.21 = (s32[]{:T(128)}, f32[8,384,384]{2,1,0:T(8,128)}, f32[8,3]{1,0:T(8,128)S(1)}, f32[8,3,384,384]{3,2,1,0:T(8,128)}, s32[8,3]{1,0:T(8,128)S(1)}, /*index=5*/f32[16,384,384]{2,1,0:T(8,128)}, s32[]{:T(128)}) while((s32[]{:T(128)}, f32[8,384,384]{2,1,0:T(8,128)}, f32[8,3]{1,0:T(8,128)S(1)}, f32[8,3,384,384]{3,2,1,0:T(8,128)}, ...), condition=%wide.region_21.25_spmd, body=%wide.region_19.24_spmd.sunk | while | flops 4078044160 | bytes 14160067 | solution.py:113
  238.8 5.2 fusion.87
  244.0 5.2 multiply_reduce_fusion.4
  254.4 5.2 fusion.87
  259.7 5.2 multiply_reduce_fusion.4
  270.1 5.2 fusion.87
  275.3 5.2 multiply_reduce_fusion.4
  285.8 5.2 fusion.87
  291.0 5.2 multiply_reduce_fusion.4
  301.4 5.2 fusion.87
  306.7 5.2 multiply_reduce_fusion.4
  317.1 5.2 fusion.87
  322.3 5.2 multiply_reduce_fusion.4
  332.7 5.2 fusion.87
  338.0 5.2 multiply_reduce_fusion.4
  348.4 5.2 fusion.87
  353.6 5.2 multiply_reduce_fusion.4
  359.7 8.0 %divide_subtract_fusion.1 = f32[8,384,384]{2,1,0:T(8,128)} fusion(f32[8,384,384]{2,1,0:T(8,128)} %param.20, f32[8,384,384]{2,1,0:T(8,128)} %get-tuple-element.100, f32[8,384,384]{2,1,0:T(8,128)} %fusion.32, f32[8]{0:T(128)S(1)} %copy-done.2, f32[8,384]{1,0:T(8,128)S(1)} %copy-done.1), kind=kLoop, calls=%fused_computation.68 | loop fusion | flops 8257536 | bytes 18886688 | tf_op jit(solution)/shard_map/sub | solution.py:115
  367.7 4.4 gather_fusion.15
  379.9 51.5 %collective-permute-done.9 = f32[4,384,384]{2,1,0:T(8,128)} collective-permute-done((f32[4,384,384]{2,1,0:T(8,128)S(1)}, f32[4,384,384]{2,1,0:T(8,128)}, u32[]{:S(2)}, u32[]{:S(2)}) %collective-permute-start.9) | collective-permute-done | bytes 2359328 | tf_op jit(solution)/shard_map/ppermute | solution.py:28
  431.4 7.6 %pad_maximum_fusion.1 = f32[16,384,384]{2,1,0:T(8,128)} fusion(f32[4,384,384]{2,1,0:T(8,128)} %collective-permute-done.9, f32[8,384,384]{2,1,0:T(8,128)} %divide_subtract_fusion.1, f32[4,384,384]{2,1,0:T(8,128)S(1)} %collective-permute-done.8), kind=kLoop, calls=%fused_computation.63 | loop fusion | flops 4718592 | bytes 18874368 | tf_op jit(solution)/shard_map/concatenate | solution.py:90
  441.6 125.3 %while.22 = (s32[]{:T(128)}, f32[8,384,384]{2,1,0:T(8,128)}, f32[8,3]{1,0:T(8,128)S(1)}, f32[8,3,384,384]{3,2,1,0:T(8,128)}, s32[8,3]{1,0:T(8,128)S(1)}, /*index=5*/f32[16,384,384]{2,1,0:T(8,128)}, s32[]{:T(128)}) while((s32[]{:T(128)}, f32[8,384,384]{2,1,0:T(8,128)}, f32[8,3]{1,0:T(8,128)S(1)}, f32[8,3,384,384]{3,2,1,0:T(8,128)}, ...), condition=%wide.region_24.28_spmd, body=%wide.region_22.27_spmd.sunk | while | flops 4078044160 | bytes 14160067 | solution.py:113
  446.0 5.2 fusion.93
  451.2 5.2 multiply_reduce_fusion.5
  461.6 5.2 fusion.93
  466.9 5.2 multiply_reduce_fusion.5
  477.3 5.2 fusion.93
  482.5 5.2 multiply_reduce_fusion.5
  492.9 5.2 fusion.93
  498.2 5.2 multiply_reduce_fusion.5
  508.6 5.2 fusion.93
  513.8 5.2 multiply_reduce_fusion.5
  524.3 5.2 fusion.93
  529.5 5.2 multiply_reduce_fusion.5
  539.9 5.2 fusion.93
  545.2 5.2 multiply_reduce_fusion.5
  555.7 5.2 fusion.93
  560.9 5.2 multiply_reduce_fusion.5
  566.9 8.0 %divide_subtract_fusion = f32[8,384,384]{2,1,0:T(8,128)} fusion(f32[8,384,384]{2,1,0:T(8,128)} %divide_subtract_fusion.1, f32[8,384,384]{2,1,0:T(8,128)} %get-tuple-element.101, f32[8,384,384]{2,1,0:T(8,128)} %fusion.32, f32[8]{0:T(128)S(1)} %copy-done.2, f32[8,384]{1,0:T(8,128)S(1)} %copy-done.1), kind=kLoop, calls=%fused_computation.67 | loop fusion | flops 8257536 | bytes 18886688 | tf_op jit(solution)/shard_map/sub | solution.py:115
  (194 shorter events, 152.0 us)
Async XLA Ops:
  0.0 25.5 %collective-permute-start.6 = (s32[8,3]{0,1:T(4,128)}, s32[8,3]{0,1:T(4,128)S(1)}, u32[]{:S(2)}, u32[]{:S(2)}) collective-permute-start(s32[8,3]{0,1:T(4,128)} %param.26), channel_id=1, source_target_pairs={{0,1},{1,2},{2,3},{3,4},{4,5},{5,6},{6,7},{7,8},{8,9},{9,10},{10,1... | collective-permute-start | bytes 296 | tf_op jit(solution)/shard_map/ppermute | solution.py:26
  2.6 27.7 %collective-permute-start.4 = (s32[8,3]{0,1:T(4,128)}, s32[8,3]{0,1:T(4,128)S(1)}, u32[]{:S(2)}, u32[]{:S(2)}) collective-permute-start(s32[8,3]{0,1:T(4,128)} %param.26), channel_id=1, source_target_pairs={{1,0},{2,1},{3,2},{4,3},{5,4},{6,5},{7,6},{8,7},{9,8},{10,9},{11,1... | collective-permute-start | bytes 296 | tf_op jit(solution)/shard_map/ppermute | solution.py:28
  2.6 153.4 %collective-permute-start = (f32[2,384,768]{2,1,0:T(8,128)}, f32[2,384,768]{2,1,0:T(8,128)}, u32[]{:S(2)}, u32[]{:S(2)}) collective-permute-start(f32[2,384,768]{2,1,0:T(8,128)} %param.19), channel_id=1, source_target_pairs={{0,2},{1,3},{2,4},{3,5},{4,6},{5,7},{6,8},{7,9},{8,10},{9,11},{10,... | collective-permute-start | bytes 7077896 | tf_op jit(solution)/shard_map/ppermute | solution.py:16
  7.3 176.3 %collective-permute-start.1 = (f32[2,384,768]{2,1,0:T(8,128)}, f32[2,384,768]{2,1,0:T(8,128)}, u32[]{:S(2)}, u32[]{:S(2)}) collective-permute-start(f32[2,384,768]{2,1,0:T(8,128)} %param.19), channel_id=1, source_target_pairs={{0,1},{1,2},{2,3},{3,4},{4,5},{5,6},{6,7},{7,8},{8,9},{9,10},{10,1... | collective-permute-start | bytes 7077896 | tf_op jit(solution)/shard_map/ppermute | solution.py:16
  10.6 177.7 %collective-permute-start.2 = (f32[2,384,768]{2,1,0:T(8,128)}, f32[2,384,768]{2,1,0:T(8,128)}, u32[]{:S(2)}, u32[]{:S(2)}) collective-permute-start(f32[2,384,768]{2,1,0:T(8,128)} %param.19), channel_id=1, source_target_pairs={{1,0},{2,1},{3,2},{4,3},{5,4},{6,5},{7,6},{8,7},{9,8},{10,9},{11,1... | collective-permute-start | bytes 7077896 | tf_op jit(solution)/shard_map/ppermute | solution.py:16
  25.5 166.1 %collective-permute-start.3 = (f32[2,384,768]{2,1,0:T(8,128)}, f32[2,384,768]{2,1,0:T(8,128)}, u32[]{:S(2)}, u32[]{:S(2)}) collective-permute-start(f32[2,384,768]{2,1,0:T(8,128)} %param.19), channel_id=1, source_target_pairs={{2,0},{3,1},{4,2},{5,3},{6,4},{7,5},{8,6},{9,7},{10,8},{11,9},{12,... | collective-permute-start | bytes 7077896 | tf_op jit(solution)/shard_map/ppermute | solution.py:16
  42.1 181.5 %collective-permute-start.7 = (f32[4,384,384]{2,1,0:T(8,128)}, f32[4,384,384]{2,1,0:T(8,128)}, u32[]{:S(2)}, u32[]{:S(2)}) collective-permute-start(f32[4,384,384]{2,1,0:T(8,128)} %broadcast_select_fusion.2), channel_id=1, source_target_pairs={{1,0},{2,1},{3,2},{4,3},{5,4},{6,5},{7,6},{8,7},{9,8},{10,9},{11,1... | collective-permute-start | bytes 7077896 | tf_op jit(solution)/shard_map/ppermute | solution.py:28
  42.1 120.8 %copy-start.3 = (f32[8,3]{0,1:T(4,128)S(1)}, f32[8,3]{0,1:T(4,128)}, u32[]{:S(2)}) copy-start(f32[8,3]{0,1:T(4,128)} %param.22) | copy-start | bytes 292
  42.1 121.0 %copy-start.4 = (s32[8,2]{0,1:T(2,128)S(1)}, s32[8,2]{0,1:T(2,128)}, u32[]{:S(2)}) copy-start(s32[8,2]{0,1:T(2,128)} %param.25) | copy-start | bytes 196
  42.1 121.0 %copy-start = (f32[2,384,768]{2,1,0:T(8,128)S(1)}, f32[2,384,768]{2,1,0:T(8,128)}, u32[]{:S(2)}) copy-start(f32[2,384,768]{2,1,0:T(8,128)} %param.19) | copy-start | bytes 7077892
  156.0 67.6 %collective-permute-start.5 = (f32[4,384,384]{2,1,0:T(8,128)}, f32[4,384,384]{2,1,0:T(8,128)}, u32[]{:S(2)}, u32[]{:S(2)}) collective-permute-start(f32[4,384,384]{2,1,0:T(8,128)} %broadcast_select_fusion.3), channel_id=1, source_target_pairs={{0,1},{1,2},{2,3},{3,4},{4,5},{5,6},{6,7},{7,8},{8,9},{9,10},{10,1... | collective-permute-start | bytes 7077896 | tf_op jit(solution)/shard_map/ppermute | solution.py:26
  234.4 125.3 %copy-start.1 = (f32[8,384]{1,0:T(8,128)S(1)}, f32[8,384]{1,0:T(8,128)}, u32[]{:S(2)}) copy-start(f32[8,384]{1,0:T(8,128)} %param.23) | copy-start | bytes 36868
  234.4 125.3 %copy-start.2 = (f32[8]{0:T(128)S(1)}, f32[8]{0:T(128)}, u32[]{:S(2)}) copy-start(f32[8]{0:T(128)} %param.24) | copy-start | bytes 100
  377.0 54.3 %collective-permute-start.9 = (f32[4,384,384]{2,1,0:T(8,128)S(1)}, f32[4,384,384]{2,1,0:T(8,128)}, u32[]{:S(2)}, u32[]{:S(2)}) collective-permute-start(f32[4,384,384]{2,1,0:T(8,128)S(1)} %broadcast_select_fusion), channel_id=1, source_target_pairs={{1,0},{2,1},{3,2},{4,3},{5,4},{6,5},{7,6},{8,7},{9,8},{10,9},{11,1... | collective-permute-start | bytes 7077896 | tf_op jit(solution)/shard_map/ppermute | solution.py:28
  377.3 54.1 %collective-permute-start.8 = (f32[4,384,384]{2,1,0:T(8,128)S(1)}, f32[4,384,384]{2,1,0:T(8,128)S(1)}, u32[]{:S(2)}, u32[]{:S(2)}) collective-permute-start(f32[4,384,384]{2,1,0:T(8,128)S(1)} %broadcast_select_fusion.1), channel_id=1, source_target_pairs={{0,1},{1,2},{2,3},{3,4},{4,5},{5,6},{6,7},{7,8},{8,9},{9,10},{10,1... | collective-permute-start | bytes 7077896 | tf_op jit(solution)/shard_map/ppermute | solution.py:26
where the time goes:
time: 577 us; the launch traced here: 575 us
  matrix products  186 us (32%)
  waiting for transfers between devices  170 us (29%)
  local copies, waits for them, and re-layouts  137 us (24%)
  other arithmetic  56.1 us (10%)
  starting transfers between devices  24.7 us (4%)
    ppermute x4, waiting for transfers between devices, shifted(): return lax.ppermute(value, axis, pairs)  118 us
    dot_general x16, matrix products, project_pair(): jnp.einsum('cab,cbe->cae', intersection, picked, precision=highest, prefe...  83.3 us
    dot_general x16, matrix products, project_pair(): jnp.einsum('cae,cfe->caf', half, intersection, precision=highest, preferr...  83 us
    gather x16, local copies, waits for them, and re-layouts, project_pair(): picked = jnp.take(nearby, chosen_rows, axis=0)  69.4 us
    ppermute x3, waiting for transfers between devices, with_halo(): lax.ppermute(head, axis, [((i + 1) % count, i) for i in range(count)])  51.5 us
    dot_general x1, matrix products, shards(): jnp.einsum('paq,pbq->pab', left, right, precision=highest, preferred_elem...  19.6 us
    sub x2, other arithmetic, shards(): current = current - residual / denominator  15.9 us
    concatenate x2, other arithmetic, shards(): jnp.concatenate([received[:half_count], current, received[half_count + pa...  15.9 us
  transfers between devices with their start and end apart: 10, of which 3 were waited for; matrix products, arithmetic and copies ran while one was open for 14% of the time, Pallas kernels for 0%

commit v1 on v0

v1 whole, which is shorter than its diff:
```python
import functools

import jax
import jax.numpy as jnp
from jax import lax
from jax.experimental import pallas as pl
from jax.experimental.pallas import tpu as pltpu
from jax.sharding import PartitionSpec as P

REACH = 2
ITERS = 2
CHUNKS = 3

f32 = jnp.float32
bf16 = jnp.bfloat16
ANY = pl.BlockSpec(memory_space=pl.ANY)
SMEM = pl.BlockSpec(memory_space=pltpu.SMEM)
VMEM = pl.BlockSpec(memory_space=pltpu.VMEM)
PARAMS = pltpu.CompilerParams(vmem_limit_bytes=63 * 1024 * 1024)

INTRA, CROSS, ORDER, START, SEND_INTRA, SEND_CROSS, EARLY, EARLY_COUNT, LEFT, RIGHT, COLUMN, SECTIONS = range(12)


def after(value, *earlier):
    return lax.optimization_barrier((value,) + earlier)[0]


def cost(flops, moved):
    return pl.CostEstimate(flops=flops // 1000, bytes_accessed=moved // 1000, transcendentals=0)


def split(x):
    hi = x.astype(bf16)
    lo = (x - hi.astype(f32)).astype(bf16)
    return hi, lo


def dot_nn(a, b):
    return lax.dot_general(a, b, (((1,), (0,)), ((), ())), preferred_element_type=f32)


def dot_nt(a, b):
    return lax.dot_general(a, b, (((1,), (1,)), ((), ())), preferred_element_type=f32)


def project(x, t, gain):
    nv = x.shape[0]
    xh, xl = split(x)
    th, tl = split(t)
    wide = dot_nn(xh, jnp.concatenate([th, tl], axis=1))
    half = wide[:, :nv] + wide[:, nv:] + dot_nn(xl, th)
    hh, hl = split(half * gain)
    wide = dot_nt(hh, jnp.concatenate([xh, xl], axis=0))
    return wide[:, :nv] + wide[:, nv:] + dot_nt(hl, xh)


def plan_kernel(devices, orbitals, where, couplings, lists_intra, lists_cross, pair_orbs, plan, seen):
    pairs = couplings.shape[0]
    half = pairs // 2
    device = where[0]
    core = device % 2
    odd = (device // 2) % 2
    partner = device + 1 - 2 * core
    outside = (device - 1 + 2 * core + devices) % devices

    def mark(lists, column, base):
        for q in range(pairs):
            seen[q] = 0
        for p in range(pairs):
            seen[lists[p, column] - base] = 1

    def ranks(lists, column, base, section):
        mark(lists, column, base)
        below = jnp.int32(0)
        for q in range(pairs):
            here = seen[q]
            seen[q] = below
            below = below + here
        for p in range(pairs):
            plan[section * pairs + p] = jnp.minimum(seen[lists[p, column] - base], half - 1)

    def sends(lists, column, section):
        mark(lists, column, device * pairs)
        below = jnp.int32(0)
        for q in range(pairs):
            here = seen[q]
            plan[section * pairs + q] = jnp.where(jnp.logical_and(here == 1, below < half), below, -1)
            below = below + here

    def sort(section, key, keys, cuts):
        filled = jnp.int32(0)
        for k in range(keys):
            if cuts is not None:
                plan[cuts * pairs + k] = filled
            for p in range(pairs):
                mine = key(p) == k

                @pl.when(mine)
                def _():
                    plan[section * pairs + filled] = p

                filled = filled + mine.astype(jnp.int32)
        if cuts is not None:
            plan[cuts * pairs + keys] = filled

    ranks(couplings, 1 - core, partner * pairs, INTRA)
    ranks(couplings, core, outside * pairs, CROSS)
    sends(lists_intra, core, SEND_INTRA)
    sends(lists_cross, 1 - core, SEND_CROSS)
    sort(ORDER, lambda p: plan[CROSS * pairs + p], half, START)

    swapped = (REACH + 1 - 2 * core) * orbitals
    near = (1 - odd) * 2 * REACH * orbitals
    late = jnp.int32(0)
    for p in range(pairs):
        right = pair_orbs[p, 1] - (device - REACH) * orbitals
        plan[LEFT * pairs + p] = pair_orbs[p, 0] - device * orbitals
        plan[RIGHT * pairs + p] = right
        first = jnp.logical_or(
            jnp.logical_and(right >= swapped, right < swapped + orbitals),
            jnp.logical_and(right >= near, right < near + orbitals),
        )
        seen[p] = 1 - first.astype(jnp.int32)
        late = late + seen[p]
    sort(EARLY, lambda p: seen[p], 2, None)
    plan[EARLY_COUNT * pairs] = pairs - late
    plan[COLUMN * pairs] = 1 - core
    plan[COLUMN * pairs + 1] = core
    plan[COLUMN * pairs + 2] = swapped
    plan[COLUMN * pairs + 3] = near
    plan[COLUMN * pairs + 4] = 2 * REACH * orbitals - near
    plan[COLUMN * pairs + 5] = 2 * REACH * orbitals - swapped


def make_plan(devices, orbitals, where, couplings, lists_intra, lists_cross, pair_orbs):
    pairs = couplings.shape[0]
    return pl.pallas_call(
        functools.partial(plan_kernel, devices, orbitals),
        out_shape=jax.ShapeDtypeStruct((SECTIONS * pairs,), jnp.int32),
        in_specs=[SMEM] * 5,
        out_specs=SMEM,
        scratch_shapes=[pltpu.SMEM((pairs,), jnp.int32)],
        name="plan",
    )(where, couplings, lists_intra, lists_cross, pair_orbs)


def send_copies(p, plan, source, cross, intra, cross_sem, intra_sem, act):
    pairs = plan.shape[0] // SECTIONS
    for section, outs, sem in ((SEND_CROSS, cross, cross_sem), (SEND_INTRA, intra, intra_sem)):
        place = plan[section * pairs + p]
        for r, out in enumerate(outs):

            @pl.when(place == r)
            def _():
                act(pltpu.make_async_copy(source, out, sem.at[r]))


def start(copy):
    copy.start()


def wait(copy):
    copy.wait()


def rank_groups(half):
    return [(0, half - 1), (half - 1, half)]


def send_shapes(half, nv):
    sizes = [high - low for low, high in rank_groups(half)] + [half]
    return [jax.ShapeDtypeStruct((size, nv, nv), f32) for size in sizes]


def send_views(half, outs):
    groups = rank_groups(half)
    cross = [outs[k].at[r] for k, (low, high) in enumerate(groups) for r in range(high - low)]
    return cross, [outs[len(groups)].at[r] for r in range(half)]


def gather_kernel(plan, current, *rest):
    outs, (rows, load_sem, cross_sem, intra_sem) = rest[:-4], rest[-4:]
    pairs = current.shape[0]
    half = pairs // 2
    cross, intra = send_views(half, outs)
    loads = [pltpu.make_async_copy(current.at[p], rows.at[p], load_sem.at[p]) for p in range(pairs)]
    for load in loads:
        load.start()
    for p in range(pairs):
        loads[p].wait()
        send_copies(p, plan, rows.at[p], cross, intra, cross_sem, intra_sem, start)
    for p in range(pairs):
        send_copies(p, plan, rows.at[p], cross, intra, cross_sem, intra_sem, wait)


def gather_rows(plan, current):
    pairs, nv, _ = current.shape
    half = pairs // 2
    outs = pl.pallas_call(
        gather_kernel,
        out_shape=send_shapes(half, nv),
        in_specs=[SMEM, ANY],
        out_specs=[ANY] * len(send_shapes(half, nv)),
        scratch_shapes=[
            pltpu.VMEM((pairs, nv, nv), f32),
            pltpu.SemaphoreType.DMA((pairs,)),
            pltpu.SemaphoreType.DMA((half,)),
            pltpu.SemaphoreType.DMA((half,)),
        ],
        compiler_params=PARAMS,
        cost_estimate=cost(0, 2 * pairs * nv * nv * 4),
        name="gather_rows",
    )(plan, current)
    return list(outs[:-1]), outs[-1]


def couple_kernel(column, plan, x, t, gain, *rest):
    p = pl.program_id(0)
    c = column if column is not None else plan[COLUMN * pl.num_programs(0)]
    value = project(x[0, 0], t[0], gain[p, c])
    rest[-1][0] = value if len(rest) == 1 else rest[0][0] + value


def couple(column, section, plan, x, t, gain, before=None):
    pairs, _, nv, _ = x.shape
    square = pl.BlockSpec((1, nv, nv), lambda p, plan: (p, 0, 0))
    which = lambda plan: column if column is not None else plan[COLUMN * pairs]
    in_specs = [
        pl.BlockSpec((1, 1, nv, nv), lambda p, plan: (p, which(plan), 0, 0)),
        pl.BlockSpec((1, nv, nv), lambda p, plan: (plan[section * pairs + p], 0, 0)),
        SMEM,
    ]
    operands = [x, t, gain]
    if before is not None:
        in_specs.append(square)
        operands.append(before)
    return pl.pallas_call(
        functools.partial(couple_kernel, column),
        out_shape=jax.ShapeDtypeStruct((pairs, nv, nv), f32),
        grid_spec=pltpu.PrefetchScalarGridSpec(
            num_scalar_prefetch=1, grid=(pairs,), in_specs=in_specs, out_specs=square
        ),
        compiler_params=PARAMS,
        cost_estimate=cost(pairs * 12 * nv**3, pairs * nv * nv * 12),
        name="couple",
    )(plan, *operands)


def finish_kernel(low, high, sending, plan, gain, occ, across, down, x, before, integral, own, *rest):
    rest, scratch = rest[:-12], rest[-12:]
    x_buf, t_buf, before_buf, integral_buf, own_buf, out_buf, sem, t_sem, out_sem, cross_sem, intra_sem, _ = scratch
    pairs = x.shape[0]
    half = pairs // 2
    t = rest[0]
    outs = rest[len(rest) - (len(rank_groups(half)) + 2 if sending else 1) :]
    out = outs[0]
    first = plan[START * pairs + low]
    count = plan[START * pairs + high] - first
    column = plan[COLUMN * pairs + 1]
    pair = lambda s: plan[ORDER * pairs + first + s]

    def fetch(s, slot):
        p = pair(s)
        return (
            pltpu.make_async_copy(x.at[p, column], x_buf.at[slot], sem.at[slot, 0]),
            pltpu.make_async_copy(before.at[p], before_buf.at[slot], sem.at[slot, 1]),
            pltpu.make_async_copy(integral.at[p], integral_buf.at[slot], sem.at[slot, 2]),
            pltpu.make_async_copy(own.at[p], own_buf.at[slot], sem.at[slot, 3]),
        )

    def stores(s, act):
        p = pair(s)
        act(pltpu.make_async_copy(out_buf.at[s], out.at[p], out_sem.at[s]))
        if sending:
            cross, intra = send_views(half, outs[1:])
            send_copies(p, plan, out_buf.at[s], cross, intra, cross_sem, intra_sem, act)

    t_copies = [pltpu.make_async_copy(t.at[k], t_buf.at[k], t_sem.at[k]) for k in range(high - low)]

    @pl.when(count > 0)
    def _():
        for copy in fetch(0, 0):
            copy.start()

    for copy in t_copies:
        copy.start()
    for copy in t_copies:
        copy.wait()

    def one(s, carry):
        slot = s % 2

        @pl.when(s + 1 < count)
        def _():
            for copy in fetch(s + 1, 1 - slot):
                copy.start()

        for copy in fetch(s, slot):
            copy.wait()
        p = pair(s)
        picked = t_buf[plan[CROSS * pairs + p] - low]
        coupled = before_buf[slot] + project(x_buf[slot], picked, gain[p, column])
        lane = lax.broadcasted_iota(jnp.int32, down.shape, 1)
        tall = jnp.sum(jnp.where(lane == p, down[...], 0.0), axis=1, keepdims=True)
        denominator = tall + across[pl.ds(p, 1), :] - occ[p]
        mine = own_buf[slot]
        residual = integral_buf[slot] + denominator * mine - coupled
        out_buf[s] = mine - residual / denominator
        stores(s, start)
        return carry

    lax.fori_loop(0, count, one, 0)

    def end(s, carry):
        stores(s, wait)
        return carry

    lax.fori_loop(0, count, end, 0)


def finish(low, high, sending, plan, x, t, gain, before, integral, own, across, down, occ, done):
    pairs, _, nv, _ = x.shape
    half = pairs // 2
    operands = [plan, gain, occ, across, down, x, before, integral, own, t]
    in_specs = [SMEM] * 3 + [VMEM] * 2 + [ANY] * 5
    out_shape = [jax.ShapeDtypeStruct((pairs, nv, nv), f32)]
    if sending:
        out_shape += send_shapes(half, nv)
    aliases = {}
    if done is not None:
        aliases = {len(operands) + k: k for k in range(len(done))}
        in_specs += [ANY] * len(done)
        operands += done
    two = pltpu.VMEM((2, nv, nv), f32)
    return pl.pallas_call(
        functools.partial(finish_kernel, low, high, sending),
        out_shape=out_shape,
        in_specs=in_specs,
        out_specs=[ANY] * len(out_shape),
        scratch_shapes=[
            two,
            pltpu.VMEM((high - low, nv, nv), f32),
            two,
            two,
            two,
            pltpu.VMEM((pairs, nv, nv), f32),
            pltpu.SemaphoreType.DMA((2, 4)),
            pltpu.SemaphoreType.DMA((high - low,)),
            pltpu.SemaphoreType.DMA((pairs,)),
            pltpu.SemaphoreType.DMA((half,)),
            pltpu.SemaphoreType.DMA((half,)),
            pltpu.SMEM((1,), jnp.int32),
        ],
        input_output_aliases=aliases,
        compiler_params=PARAMS,
        cost_estimate=cost(2 * (high - low) * 12 * nv**3, 2 * (high - low) * nv * nv * 24),
        name="finish",
    )(*operands)


def integrals_kernel(early, wholes, pieces, plan, slabs, *rest):
    rest, (left_buf, high, low, right_buf, out_buf, left_sem, right_sem, out_sem) = rest[:-8], rest[-8:]
    out = rest[-1]
    orbitals, nv, nq = slabs.shape
    pairs = out.shape[0]
    per = pieces
    rows = nv // per
    bases = plan[COLUMN * pairs + 2], plan[COLUMN * pairs + 3], plan[COLUMN * pairs + 4], plan[COLUMN * pairs + 5]
    sources = []
    if wholes:
        whole = rest[0]
        sources.append((bases[0], [[whole.at[o, pl.ds(k * rows, rows)] for k in range(per)] for o in range(orbitals)]))
    used = wholes
    for base in ((bases[1],) if early else (bases[2], bases[3])):
        refs = rest[used : used + pieces]
        used += pieces
        sources.append((base, [[refs[k].at[o] for k in range(per)] for o in range(orbitals)]))
    count = plan[EARLY_COUNT * pairs] if early else pairs - plan[EARLY_COUNT * pairs]
    first = 0 if early else plan[EARLY_COUNT * pairs]
    pair = lambda s: plan[EARLY * pairs + first + s]

    def fetch(s, slot):
        right = plan[RIGHT * pairs + pair(s)]
        for base, held in sources:
            for o in range(orbitals):

                @pl.when(right == base + o)
                def _():
                    for k in range(per):
                        target = right_buf.at[slot, pl.ds(k * rows, rows)]
                        pltpu.make_async_copy(held[o][k], target, right_sem.at[slot, k]).start()

    def arrived(slot):
        for k in range(per):
            target = right_buf.at[slot, pl.ds(k * rows, rows)]
            pltpu.make_async_copy(slabs.at[0, pl.ds(k * rows, rows)], target, right_sem.at[slot, k]).wait()

    def store(s, slot):
        return pltpu.make_async_copy(out_buf.at[slot], out.at[pair(s)], out_sem.at[slot])

    lefts = [pltpu.make_async_copy(slabs.at[o], left_buf.at[o], left_sem.at[o]) for o in range(orbitals)]
    for copy in lefts:
        copy.start()

    @pl.when(count > 0)
    def _():
        fetch(0, 0)

    for o in range(orbitals):
        lefts[o].wait()
        high[o], low[o] = split(left_buf[o])

    def one(s, carry):
        slot = s % 2

        @pl.when(s + 1 < count)
        def _():
            fetch(s + 1, 1 - slot)

        arrived(slot)

        @pl.when(s >= 2)
        def _():
            store(s - 2, slot).wait()

        left = plan[LEFT * pairs + pair(s)]
        rh, rl = split(right_buf[slot])
        wide = dot_nt(high[left], jnp.concatenate([rh, rl], axis=0))
        out_buf[slot] = wide[:, :nv] + wide[:, nv:] + dot_nt(low[left], rh)
        store(s, slot).start()
        return carry

    lax.fori_loop(0, count, one, 0)

    @pl.when(count >= 2)
    def _():
        store(count - 2, count % 2).wait()

    @pl.when(count >= 1)
    def _():
        store(count - 1, (count + 1) % 2).wait()


def pair_integrals(early, plan, slabs, pairs, wholes, pieces, done=None):
    orbitals, nv, nq = slabs.shape
    operands = [plan, slabs, *wholes]
    for group in pieces:
        operands += group
    in_specs = [SMEM] + [ANY] * (len(operands) - 1)
    aliases = {}
    if done is not None:
        aliases = {len(operands): 0}
        operands.append(done)
        in_specs.append(ANY)
    return pl.pallas_call(
        functools.partial(integrals_kernel, early, len(wholes), len(pieces[0])),
        out_shape=jax.ShapeDtypeStruct((pairs, nv, nv), f32),
        in_specs=in_specs,
        out_specs=ANY,
        scratch_shapes=[
            pltpu.VMEM((orbitals, nv, nq), f32),
            pltpu.VMEM((orbitals, nv, nq), bf16),
            pltpu.VMEM((orbitals, nv, nq), bf16),
            pltpu.VMEM((2, nv, nq), f32),
            pltpu.VMEM((2, nv, nv), f32),
            pltpu.SemaphoreType.DMA((orbitals,)),
            pltpu.SemaphoreType.DMA((2, len(pieces[0]))),
            pltpu.SemaphoreType.DMA((2,)),
        ],
        input_output_aliases=aliases,
        compiler_params=PARAMS,
        cost_estimate=cost(pairs * 3 * nv * nv * nq, pairs * 2 * nv * nq),
        name="pair_integrals",
    )(*operands)


def shards(slabs, amplitudes, intersections, fock_coupling, virt_energy, occ_pair_energy, pair_orbs, couplings):
    axis = "orb"
    count = lax.axis_size(axis)
    device = lax.axis_index(axis)
    selects_near = device % 2 == (device // 2) % 2
    orbitals, nv, nq = slabs.shape
    pairs = amplitudes.shape[0]
    half = pairs // 2

    everyone = range(count)
    chip_odd = lambda i: (i // 2) % 2
    inside = [(i, i ^ 1) for i in everyone]
    beside = [(i, (i + 1) % count if i % 2 else (i - 1) % count) for i in everyone]
    near_perm = [(i, i ^ 2) for i in everyone]
    far_perm = [(i, (i - 4 if chip_odd(i) else i + 4) % count) for i in everyone]
    send = lambda value, perm: lax.ppermute(value, axis, perm)

    lists_intra = send(couplings, inside)
    lists_cross = send(couplings, beside)
    rows = nv // CHUNKS
    pieces = [slabs[:, k * rows : (k + 1) * rows] for k in range(CHUNKS)]
    *pieces, lists_intra, lists_cross = lax.optimization_barrier((*pieces, lists_intra, lists_cross))
    near = [send(piece, near_perm) for piece in pieces]

    own_row = couplings[:, 2] - device * pairs
    partial = couple(2, 0, after(own_row, *pieces), intersections, amplitudes, fock_coupling)
    near[0], partial = lax.optimization_barrier((near[0], partial))
    far = [send(near[0], far_perm)]

    where = after(device.astype(jnp.int32).reshape(1), partial)
    plan = make_plan(count, orbitals, where, couplings, lists_intra, lists_cross, pair_orbs)
    across, down = virt_energy, virt_energy.T
    cross_out, intra_out = gather_rows(plan, amplitudes)
    intra_t = send(intra_out, inside)
    slabs_swapped = send(after(slabs, intra_out), inside)

    near[1], intra_out = lax.optimization_barrier((near[1], intra_out))
    far.append(send(near[1], far_perm))
    partial = couple(None, INTRA, plan, intersections, intra_t, fock_coupling, after(partial, near[1]))
    near[2], far[0], partial, *cross_out = lax.optimization_barrier((near[2], far[0], partial, *cross_out))
    cross_t = [send(rows_out, beside) for rows_out in cross_out]
    far.append(send(near[2], far_perm))
    relayed = [send(jnp.where(selects_near, n, f), inside) for n, f in zip(near, far)]
    integrals = pair_integrals(True, plan, after(slabs, partial), pairs, [slabs_swapped], [near])
    integrals = pair_integrals(False, plan, slabs, pairs, [], [far, relayed], integrals)

    current = amplitudes
    for iteration in range(ITERS):
        if iteration > 0:
            cross_t = [send(rows_out, beside) for rows_out in cross_out]
            intra_t = send(intra_out, inside)
            partial = couple(2, 0, own_row, intersections, current, fock_coupling)
            partial = couple(None, INTRA, plan, intersections, intra_t, fock_coupling, partial)
        sending = iteration + 1 < ITERS
        done = None
        for k, (low, high) in enumerate(rank_groups(half)):
            done = finish(
                low,
                high,
                sending,
                plan,
                intersections,
                cross_t[k],
                fock_coupling,
                partial,
                integrals,
                current,
                across,
                down,
                occ_pair_energy,
                done,
            )
        current = done[0]
        if sending:
            cross_out, intra_out = done[1:-1], done[-1]
    return current


def solution(mesh):
    in_specs = (
        P("orb", None, None),
        P("orb", None, None),
        P("orb", None, None, None),
        P("orb", None),
        P("orb", None),
        P("orb"),
        P("orb", None),
        P("orb", None),
    )
    out_specs = P("orb", None, None)
    return jax.shard_map(shards, mesh=mesh, in_specs=in_specs, out_specs=out_specs, check_vma=False)
```

time: 577 us -> 222 us (0.38)
  matrix products: 186 us -> 0 us
  local copies, waits for them, and re-layouts: 137 us -> 8.67 us
  Pallas kernels: 0 us -> 117 us
  waiting for transfers between devices: 170 us -> 66.7 us
  other arithmetic: 56.1 us -> 5.27 us
    dot_general x33 -> x0, matrix products: 186 us -> none  [the longest x16 83.3 us: project_pair(): jnp.einsum('cab,cbe->cae', intersection, picked, precision=highest, prefe...]
    pallas_call x0 -> x12, Pallas kernels: none -> 117 us  [the longest x4 54.4 us: couple(): pl.pallas_call(functools.partial(couple_kernel, column), out_shape=jax.Sh...]
    gather x30 -> x0, local copies, waits for them, and re-layouts: 104 us -> none  [the longest x16 69.4 us: project_pair(): picked = jnp.take(nearby, chosen_rows, axis=0)]
    ppermute x10 -> x18, waiting for transfers between devices: 170 us -> 66.7 us  [shards(): send = lambda value, perm: lax.ppermute(value, axis, perm)]
    concatenate x2 -> x0, other arithmetic: 15.9 us -> none  [shards(): jnp.concatenate([received[:half_count], current, received[half_count + pa...]
    sub x2 -> x1, other arithmetic: 15.9 us -> 1.16 us  [shards(): own_row = couplings[:, 2] - device * pairs]
    dynamic_update_slice x16 -> x0, local copies, waits for them, and re-layouts: 13.8 us -> none  [shards(): lax.map(project_pair, (coupled_index, fock_coupling, intersections))]
    select_n x22 -> x3, other arithmetic: 11.5 us -> 4.11 us  [shards(): jnp.where(selects_near, n, f)]
  transfers between devices with their start and end apart: 10 -> 18, of which waited for: 3 -> 6; matrix products, arithmetic and copies ran while one was open for 14% -> 5% of each run, Pallas kernels for 0% -> 44%
where the time goes in v1:
time: 222 us; the launch traced here: 220 us
  Pallas kernels  117 us (53%)
  waiting for transfers between devices  66.7 us (30%)
  starting transfers between devices  22.4 us (10%)
  local copies, waits for them, and re-layouts  8.67 us (4%)
  other arithmetic  5.27 us (2%)
    ppermute x18, waiting for transfers between devices, shards(): send = lambda value, perm: lax.ppermute(value, axis, perm)  66.7 us
    pallas_call x4, Pallas kernels, couple(): pl.pallas_call(functools.partial(couple_kernel, column), out_shape=jax.Sh...  54.4 us
    pallas_call x4, Pallas kernels, finish(): pl.pallas_call(functools.partial(finish_kernel, low, high, sending), out_...  39.4 us
    ppermute x18, starting transfers between devices, shards(): send = lambda value, perm: lax.ppermute(value, axis, perm)  22.4 us
    pallas_call x2, Pallas kernels, pair_integrals(): pl.pallas_call(functools.partial(integrals_kernel, early, len(wholes), le...  16.4 us
    unnamed x28, local copies, waits for them, and re-layouts  5.55 us
    pallas_call x1, Pallas kernels, gather_rows(): pl.pallas_call(gather_kernel, out_shape=send_shapes(half, nv), in_specs=[...  5 us
  transfers between devices with their start and end apart: 18, of which 6 were waited for; matrix products, arithmetic and copies ran while one was open for 5% of the time, Pallas kernels for 44%

profile of v1, /device:TPU:1, one launch (start us, length us, event | category | flops | bytes accessed | tf_op | source)
XLA Modules:
  0.0 220.2 jit_solution(8629195843888447277)
XLA Ops:
  0.0 0.8 copy.15.couplings
  0.8 2.6 %collective-permute-start.1 = (s32[8,3]{1,0:T(8,128)S(1)}, s32[8,3]{1,0:T(8,128)S(1)}, u32[]{:S(2)}, u32[]{:S(2)}) collective-permute-start(s32[8,3]{1,0:T(8,128)S(1)} %copy.15.couplings), channel_id=1, source_target_pairs={{0,31},{1,2},{2,1},{3,4},{4,3},{5,6},{6,5},{7,8},{8,7},{9,10},{10,... | collective-permute-start | bytes 296 | tf_op jit(solution)/shard_map/ppermute | solution.py:492
  3.4 3.8 %collective-permute-start = (s32[8,3]{1,0:T(8,128)S(1)}, s32[8,3]{1,0:T(8,128)S(1)}, u32[]{:S(2)}, u32[]{:S(2)}) collective-permute-start(s32[8,3]{1,0:T(8,128)S(1)} %copy.15.couplings), channel_id=1, source_target_pairs={{0,1},{1,0},{2,3},{3,2},{4,5},{5,4},{6,7},{7,6},{8,9},{9,8},{10,11... | collective-permute-start | bytes 296 | tf_op jit(solution)/shard_map/ppermute | solution.py:492
  7.2 3.1 %fusion = (f32[2,128,768]{2,1,0:T(8,128)}, f32[2,128,768]{2,1,0:T(8,128)}, f32[2,128,768]{2,1,0:T(8,128)}) fusion(f32[2,384,768]{2,1,0:T(8,128)} %slabs.2), kind=kLoop, calls=%fused_computation.4 | loop fusion | bytes 4718592 | tf_op jit(solution)/shard_map/slice | solution.py:497
  10.3 0.0 collective-permute-done.lists_intra
  10.4 0.1 collective-permute-start.2
  10.5 0.7 copy.17.gain
  11.1 0.7 copy.19.pair_orbs
  11.8 1.2 subtract_bitcast_fusion.plan
  13.0 13.2 %couple.4.rest_0_ = f32[8,384,384]{2,1,0:T(8,128)} custom-call(s32[8]{0:T(128)} %subtract_bitcast_fusion.plan, f32[8,3,384,384]{3,2,1,0:T(8,128)} %x.15, f32[8,384,384]{2,1,0:T(8,128)} %own.3, f32[8,3]{1,0:T(8,128)} %copy.17.gain), custom_call_target="tpu_custom_call" | custom-call | flops 5435817 | bytes 14155 | tf_op jit(solution)/shard_map/couple/pallas_call | solution.py:237
  26.1 3.7 %collective-permute-done.2.rest_1_ = f32[2,128,768]{2,1,0:T(8,128)S(1)} collective-permute-done((f32[2,128,768]{2,1,0:T(8,128)}, f32[2,128,768]{2,1,0:T(8,128)S(1)}, u32[]{:S(2)}, u32[]{:S(2)}) %collective-permute-start.2) | collective-permute-done | bytes 786464 | tf_op jit(solution)/shard_map/ppermute | solution.py:492
  29.8 1.8 plan.1
  31.6 5.0 %gather_rows.1 = (f32[3,384,384]{2,1,0:T(8,128)}, f32[1,384,384]{2,1,0:T(8,128)}, f32[4,384,384]{2,1,0:T(8,128)}) custom-call(s32[88]{0:T(128)} %plan.1, f32[8,384,384]{2,1,0:T(8,128)} %own.3), custom_call_target="tpu_custom_call" | custom-call | bytes 9437 | tf_op jit(solution)/shard_map/gather_rows/pallas_call | solution.py:199
  36.6 0.2 collective-permute-start.5
  36.8 0.0 collective-permute-start.6
  36.8 0.5 collective-permute-start.12
  37.4 1.6 collective-permute-start.3
  38.9 17.0 %collective-permute-done.6.rest_2_ = f32[2,128,768]{2,1,0:T(8,128)} collective-permute-done((f32[2,128,768]{2,1,0:T(8,128)}, f32[2,128,768]{2,1,0:T(8,128)}, u32[]{:S(2)}, u32[]{:S(2)}) %collective-permute-start.6) | collective-permute-done | bytes 786464 | tf_op jit(solution)/shard_map/ppermute | solution.py:492
  55.9 14.0 %couple.5.before = f32[8,384,384]{2,1,0:T(8,128)} custom-call(s32[88]{0:T(128)} %plan.1, f32[8,3,384,384]{3,2,1,0:T(8,128)} %x.15, f32[4,384,384]{2,1,0:T(8,128)} %collective-permute-done.5.t, f32[8,3]{1,0:T(8,128)} %copy.17.gain, f32[8,384,384]{2,1,0:T(8,128)} %couple.4.rest_0_), custom_call_target="tpu_custom_call" | custom-call | flops 5435817 | bytes 14155 | tf_op jit(solution)/shard_map/couple/pallas_call | solution.py:237
  69.9 2.8 %collective-permute-done.3.rest_3_ = f32[2,128,768]{2,1,0:T(8,128)} collective-permute-done((f32[2,128,768]{2,1,0:T(8,128)}, f32[2,128,768]{2,1,0:T(8,128)}, u32[]{:S(2)}, u32[]{:S(2)}) %collective-permute-start.3) | collective-permute-done | bytes 786464 | tf_op jit(solution)/shard_map/ppermute | solution.py:492
  72.8 0.0 collective-permute-start.8
  72.8 2.8 %collective-permute-start.14 = (f32[3,384,384]{2,1,0:T(8,128)}, f32[3,384,384]{2,1,0:T(8,128)}, u32[]{:S(2)}, u32[]{:S(2)}) collective-permute-start(f32[3,384,384]{2,1,0:T(8,128)} %get-tuple-element.54), channel_id=1, source_target_pairs={{0,31},{1,2},{2,1},{3,4},{4,3},{5,6},{6,5},{7,8},{8,7},{9,10},{10,... | collective-permute-start | bytes 5308424 | tf_op jit(solution)/shard_map/ppermute | solution.py:492
  75.6 0.4 collective-permute-done.7.rest_1_
  76.0 2.1 broadcast_select_fusion.1
  78.1 2.9 %collective-permute-start.10 = (f32[2,128,768]{2,1,0:T(8,128)}, f32[2,128,768]{2,1,0:T(8,128)}, u32[]{:S(2)}, u32[]{:S(2)}) collective-permute-start(f32[2,128,768]{2,1,0:T(8,128)} %broadcast_select_fusion.1), channel_id=1, source_target_pairs={{0,1},{1,0},{2,3},{3,2},{4,5},{5,4},{6,7},{7,6},{8,9},{9,8},{10,11... | collective-permute-start | bytes 2359304 | tf_op jit(solution)/shard_map/ppermute | solution.py:492
  81.0 1.0 broadcast_select_fusion.2
  82.0 0.0 collective-permute-start.9
  82.0 25.6 %collective-permute-done.8.rest_2_ = f32[2,128,768]{2,1,0:T(8,128)S(1)} collective-permute-done((f32[2,128,768]{2,1,0:T(8,128)}, f32[2,128,768]{2,1,0:T(8,128)S(1)}, u32[]{:S(2)}, u32[]{:S(2)}) %collective-permute-start.8) | collective-permute-done | bytes 786464 | tf_op jit(solution)/shard_map/ppermute | solution.py:492
  107.7 0.9 copy-done.1
  108.6 1.0 broadcast_select_fusion
  109.5 5.5 %collective-permute-start.11 = (f32[2,128,768]{2,1,0:T(8,128)}, f32[2,128,768]{2,1,0:T(8,128)S(1)}, u32[]{:S(2)}, u32[]{:S(2)}) collective-permute-start(f32[2,128,768]{2,1,0:T(8,128)} %broadcast_select_fusion), channel_id=1, source_target_pairs={{0,1},{1,0},{2,3},{3,2},{4,5},{5,4},{6,7},{7,6},{8,9},{9,8},{10,11... | collective-permute-start | bytes 2359304 | tf_op jit(solution)/shard_map/ppermute | solution.py:492
  115.0 0.8 copy.20
  115.8 11.9 %pair_integrals.2.rest_6_ = f32[8,384,384]{2,1,0:T(8,128)} custom-call(s32[88]{0:T(128)} %plan.1, f32[2,384,768]{2,1,0:T(8,128)} %slabs.2, f32[2,384,768]{2,1,0:T(8,128)} %collective-permute-done.12.rest_0_, f32[2,128,768]{2,1,0:T(8,128)} %copy-done.2, f32[2,128,768]{2,1,0:T(8,128)} %collective-permute-done.6.rest_2_, ...), custom_call_target="tpu_custom_call" | custom-call | flops 2717908 | bytes 4718 | tf_op jit(solution)/shard_map/pair_integrals/pallas_call | solution.py:455
  127.7 0.0 collective-permute-done.10.rest_4_
  127.8 0.0 collective-permute-done.9.rest_3_
  127.8 0.9 copy-done.4
  128.7 4.5 %pair_integrals.3.integral = f32[8,384,384]{2,1,0:T(8,128)} custom-call(s32[88]{0:T(128)} %plan.1, f32[2,384,768]{2,1,0:T(8,128)} %slabs.2, f32[2,128,768]{2,1,0:T(8,128)} %copy-done, f32[2,128,768]{2,1,0:T(8,128)} %collective-permute-done.7.rest_1_, f32[2,128,768]{2,1,0:T(8,128)} %copy-done.1, ...), custom_call_target="tpu_custom_call", output_to_operand_aliasing={{}: (8, {})} | custom-call | flops 2717908 | bytes 4718 | tf_op jit(solution)/shard_map/pair_integrals/pallas_call | solution.py:455
  133.2 14.2 %finish.4 = (f32[8,384,384]{2,1,0:T(8,128)}, f32[3,384,384]{2,1,0:T(8,128)}, f32[1,384,384]{2,1,0:T(8,128)}, f32[4,384,384]{2,1,0:T(8,128)}) custom-call(s32[88]{0:T(128)} %plan.1, f32[8,3]{1,0:T(8,128)} %copy.17.gain, f32[8]{0:T(128)} %occ.7, f32[8,384]{1,0:T(8,128)} %across.7, f32[384,8]{1,0:T(8,128)} %bitcast.4, f32[8,3,384,384]{3,2,1,0:T(8,128)} %x.15, ...), custom_call_target="tpu_custom_call" | custom-call | flops 4076863 | bytes 21233 | tf_op jit(solution)/shard_map/finish/pallas_call | solution.py:335
  147.4 6.2 %finish.5 = (f32[8,384,384]{2,1,0:T(8,128)}, f32[3,384,384]{2,1,0:T(8,128)}, f32[1,384,384]{2,1,0:T(8,128)}, f32[4,384,384]{2,1,0:T(8,128)}) custom-call(s32[88]{0:T(128)} %plan.1, f32[8,3]{1,0:T(8,128)} %copy.17.gain, f32[8]{0:T(128)} %occ.7, f32[8,384]{1,0:T(8,128)} %across.7, ...), custom_call_target="tpu_custom_call", output_to_operand_aliasing={{0}: (10, {}), {1}: (11, {}), {2}: (12, {}), {3}: (13, {})} | custom-call | flops 1358954 | bytes 7077 | tf_op jit(solution)/shard_map/finish/pallas_call | solution.py:335
  153.6 0.3 collective-permute-start.15
  153.9 2.0 collective-permute-start.17
  155.9 0.1 collective-permute-start.16
  156.0 13.2 %couple.6.rest_0_ = f32[8,384,384]{2,1,0:T(8,128)} custom-call(s32[8]{0:T(128)} %subtract_bitcast_fusion.plan, f32[8,3,384,384]{3,2,1,0:T(8,128)} %x.15, f32[8,384,384]{2,1,0:T(8,128)} %get-tuple-element.60.t.own, f32[8,3]{1,0:T(8,128)} %copy.17.gain), custom_call_target="tpu_custom_call" | custom-call | flops 5435817 | bytes 14155 | tf_op jit(solution)/shard_map/couple/pallas_call | solution.py:237
  169.2 14.0 %couple.7.before = f32[8,384,384]{2,1,0:T(8,128)} custom-call(s32[88]{0:T(128)} %plan.1, f32[8,3,384,384]{3,2,1,0:T(8,128)} %x.15, f32[4,384,384]{2,1,0:T(8,128)} %collective-permute-done.15.t, f32[8,3]{1,0:T(8,128)} %copy.17.gain, f32[8,384,384]{2,1,0:T(8,128)} %couple.6.rest_0_), custom_call_target="tpu_custom_call" | custom-call | flops 5435817 | bytes 14155 | tf_op jit(solution)/shard_map/couple/pallas_call | solution.py:237
  183.2 17.1 %collective-permute-done.17.rest_0_ = f32[3,384,384]{2,1,0:T(8,128)} collective-permute-done((f32[3,384,384]{2,1,0:T(8,128)}, f32[3,384,384]{2,1,0:T(8,128)}, u32[]{:S(2)}, u32[]{:S(2)}) %collective-permute-start.17) | collective-permute-done | bytes 1769504 | tf_op jit(solution)/shard_map/ppermute | solution.py:492
  200.3 12.8 %finish.6.rest_1_ = f32[8,384,384]{2,1,0:T(8,128)} custom-call(s32[88]{0:T(128)} %plan.1, f32[8,3]{1,0:T(8,128)} %copy.17.gain, f32[8]{0:T(128)} %occ.7, f32[8,384]{1,0:T(8,128)} %across.7, f32[384,8]{1,0:T(8,128)} %bitcast.6, f32[8,3,384,384]{3,2,1,0:T(8,128)} %x.15, f32[8,384,384]{2,1,0:T(8,128)} %couple.7.before, f32[8,384,384]{2,1,0:T(8,128)} %pair_integrals.3.integral, ...), custom_call_target="tpu_custom_call" | custom-call | flops 4076863 | bytes 21233 | tf_op jit(solution)/shard_map/finish/pallas_call | solution.py:335
  213.1 0.8 copy-done.5
  213.9 6.2 %finish.7 = f32[8,384,384]{2,1,0:T(8,128)} custom-call(s32[88]{0:T(128)} %plan.1, f32[8,3]{1,0:T(8,128)} %copy.17.gain, f32[8]{0:T(128)} %occ.7, f32[8,384]{1,0:T(8,128)} %across.7, f32[384,8]{1,0:T(8,128)} %bitcast.7, f32[8,3,384,384]{3,2,1,0:T(8,128)} %x.15, f32[8,384,384]{2,1,0:T(8,128)} %couple.7.before, ...), custom_call_target="tpu_custom_call", output_to_operand_aliasing={{}: (10, {})} | custom-call | flops 1358954 | bytes 7077 | tf_op jit(solution)/shard_map/finish/pallas_call | solution.py:335
  (33 shorter events, 0.1 us)
Async XLA Ops:
  0.8 9.6 %copy-start.7 = (s32[8,3]{1,0:T(8,128)}, s32[8,3]{1,0:T(8,128)S(1)}, u32[]{:S(2)}) copy-start(s32[8,3]{1,0:T(8,128)S(1)} %copy.15.couplings) | copy-start | bytes 292
  0.8 9.7 %copy-start.10 = (f32[8,3]{0,1:T(4,128)S(1)}, f32[8,3]{0,1:T(4,128)}, u32[]{:S(2)}) copy-start(f32[8,3]{0,1:T(4,128)} %param.11) | copy-start | bytes 292
  0.8 10.4 %copy-start.11 = (s32[8,2]{0,1:T(2,128)S(1)}, s32[8,2]{0,1:T(2,128)}, u32[]{:S(2)}) copy-start(s32[8,2]{0,1:T(2,128)} %param.14) | copy-start | bytes 196
  0.8 9.6 %collective-permute-start.1 = (s32[8,3]{1,0:T(8,128)S(1)}, s32[8,3]{1,0:T(8,128)S(1)}, u32[]{:S(2)}, u32[]{:S(2)}) collective-permute-start(s32[8,3]{1,0:T(8,128)S(1)} %copy.15.couplings), channel_id=1, source_target_pairs={{0,31},{1,2},{2,1},{3,4},{4,3},{5,6},{6,5},{7,8},{8,7},{9,10},{10,... | collective-permute-start | bytes 296 | tf_op jit(solution)/shard_map/ppermute | solution.py:492
  3.4 7.0 %collective-permute-start = (s32[8,3]{1,0:T(8,128)S(1)}, s32[8,3]{1,0:T(8,128)S(1)}, u32[]{:S(2)}, u32[]{:S(2)}) collective-permute-start(s32[8,3]{1,0:T(8,128)S(1)} %copy.15.couplings), channel_id=1, source_target_pairs={{0,1},{1,0},{2,3},{3,2},{4,5},{5,4},{6,7},{7,6},{8,9},{9,8},{10,11... | collective-permute-start | bytes 296 | tf_op jit(solution)/shard_map/ppermute | solution.py:492
  10.3 15.8 %copy-start.8 = (s32[8,3]{1,0:T(8,128)}, s32[8,3]{1,0:T(8,128)S(1)}, u32[]{:S(2)}) copy-start(s32[8,3]{1,0:T(8,128)S(1)} %collective-permute-done.1.lists_cross) | copy-start | bytes 292
  10.4 15.8 %copy-start.9 = (s32[8,3]{1,0:T(8,128)}, s32[8,3]{1,0:T(8,128)S(1)}, u32[]{:S(2)}) copy-start(s32[8,3]{1,0:T(8,128)S(1)} %collective-permute-done.lists_intra) | copy-start | bytes 292
  10.4 19.4 %collective-permute-start.2 = (f32[2,128,768]{2,1,0:T(8,128)}, f32[2,128,768]{2,1,0:T(8,128)S(1)}, u32[]{:S(2)}, u32[]{:S(2)}) collective-permute-start(f32[2,128,768]{2,1,0:T(8,128)} %get-tuple-element.34), channel_id=1, source_target_pairs={{0,2},{1,3},{2,0},{3,1},{4,6},{5,7},{6,4},{7,5},{8,10},{9,11},{10,... | collective-permute-start | bytes 2359304 | tf_op jit(solution)/shard_map/ppermute | solution.py:492
  29.8 6.8 %copy-start.2 = (f32[2,128,768]{2,1,0:T(8,128)}, f32[2,128,768]{2,1,0:T(8,128)S(1)}, u32[]{:S(2)}) copy-start(f32[2,128,768]{2,1,0:T(8,128)S(1)} %collective-permute-done.2.rest_1_) | copy-start | bytes 2359300
  36.6 19.3 %collective-permute-start.5 = (f32[4,384,384]{2,1,0:T(8,128)}, f32[4,384,384]{2,1,0:T(8,128)}, u32[]{:S(2)}, u32[]{:S(2)}) collective-permute-start(f32[4,384,384]{2,1,0:T(8,128)} %get-tuple-element.43), channel_id=1, source_target_pairs={{0,1},{1,0},{2,3},{3,2},{4,5},{5,4},{6,7},{7,6},{8,9},{9,8},{10,11... | collective-permute-start | bytes 7077896 | tf_op jit(solution)/shard_map/ppermute | solution.py:492
  36.8 19.1 %collective-permute-start.6 = (f32[2,128,768]{2,1,0:T(8,128)}, f32[2,128,768]{2,1,0:T(8,128)}, u32[]{:S(2)}, u32[]{:S(2)}) collective-permute-start(f32[2,128,768]{2,1,0:T(8,128)} %get-tuple-element.35), channel_id=1, source_target_pairs={{0,2},{1,3},{2,0},{3,1},{4,6},{5,7},{6,4},{7,5},{8,10},{9,11},{10,... | collective-permute-start | bytes 2359304 | tf_op jit(solution)/shard_map/ppermute | solution.py:492
  36.8 78.2 %collective-permute-start.12 = (f32[2,384,768]{2,1,0:T(8,128)}, f32[2,384,768]{2,1,0:T(8,128)}, u32[]{:S(2)}, u32[]{:S(2)}) collective-permute-start(f32[2,384,768]{2,1,0:T(8,128)} %slabs.2), channel_id=1, source_target_pairs={{0,1},{1,0},{2,3},{3,2},{4,5},{5,4},{6,7},{7,6},{8,9},{9,8},{10,11... | collective-permute-start | bytes 7077896 | tf_op jit(solution)/shard_map/ppermute | solution.py:492
  37.4 35.4 %collective-permute-start.3 = (f32[2,128,768]{2,1,0:T(8,128)}, f32[2,128,768]{2,1,0:T(8,128)}, u32[]{:S(2)}, u32[]{:S(2)}) collective-permute-start(f32[2,128,768]{2,1,0:T(8,128)} %get-tuple-element.36), channel_id=1, source_target_pairs={{0,2},{1,3},{2,0},{3,1},{4,6},{5,7},{6,4},{7,5},{8,10},{9,11},{10,... | collective-permute-start | bytes 2359304 | tf_op jit(solution)/shard_map/ppermute | solution.py:492
  38.9 33.8 %collective-permute-start.4 = (f32[2,128,768]{2,1,0:T(8,128)}, f32[2,128,768]{2,1,0:T(8,128)S(1)}, u32[]{:S(2)}, u32[]{:S(2)}) collective-permute-start(f32[2,128,768]{2,1,0:T(8,128)} %copy-done.2), channel_id=1, source_target_pairs={{0,4},{1,5},{2,30},{3,31},{4,8},{5,9},{6,2},{7,3},{8,12},{9,13},{1... | collective-permute-start | bytes 2359304 | tf_op jit(solution)/shard_map/ppermute | solution.py:492
  55.9 20.1 %collective-permute-start.7 = (f32[2,128,768]{2,1,0:T(8,128)}, f32[2,128,768]{2,1,0:T(8,128)}, u32[]{:S(2)}, u32[]{:S(2)}) collective-permute-start(f32[2,128,768]{2,1,0:T(8,128)} %collective-permute-done.6.rest_2_), channel_id=1, source_target_pairs={{0,4},{1,5},{2,30},{3,31},{4,8},{5,9},{6,2},{7,3},{8,12},{9,13},{1... | collective-permute-start | bytes 2359304 | tf_op jit(solution)/shard_map/ppermute | solution.py:492
  69.9 11.1 %copy-start.3 = (f32[2,128,768]{2,1,0:T(8,128)S(1)}, f32[2,128,768]{2,1,0:T(8,128)}, u32[]{:S(2)}) copy-start(f32[2,128,768]{2,1,0:T(8,128)} %copy-done.2) | copy-start | bytes 2359300
  72.8 9.2 %copy-start = (f32[2,128,768]{2,1,0:T(8,128)}, f32[2,128,768]{2,1,0:T(8,128)S(1)}, u32[]{:S(2)}) copy-start(f32[2,128,768]{2,1,0:T(8,128)S(1)} %collective-permute-done.4.rest_0_) | copy-start | bytes 2359300
  72.8 34.9 %collective-permute-start.8 = (f32[2,128,768]{2,1,0:T(8,128)}, f32[2,128,768]{2,1,0:T(8,128)S(1)}, u32[]{:S(2)}, u32[]{:S(2)}) collective-permute-start(f32[2,128,768]{2,1,0:T(8,128)} %collective-permute-done.3.rest_3_), channel_id=1, source_target_pairs={{0,4},{1,5},{2,30},{3,31},{4,8},{5,9},{6,2},{7,3},{8,12},{9,13},{1... | collective-permute-start | bytes 2359304 | tf_op jit(solution)/shard_map/ppermute | solution.py:492
  72.8 60.4 %collective-permute-start.14 = (f32[3,384,384]{2,1,0:T(8,128)}, f32[3,384,384]{2,1,0:T(8,128)}, u32[]{:S(2)}, u32[]{:S(2)}) collective-permute-start(f32[3,384,384]{2,1,0:T(8,128)} %get-tuple-element.54), channel_id=1, source_target_pairs={{0,31},{1,2},{2,1},{3,4},{4,3},{5,6},{6,5},{7,8},{8,7},{9,10},{10,... | collective-permute-start | bytes 5308424 | tf_op jit(solution)/shard_map/ppermute | solution.py:492
  78.1 36.9 %copy-start.6 = (f32[8,384]{1,0:T(8,128)S(1)}, f32[8,384]{1,0:T(8,128)}, u32[]{:S(2)}) copy-start(f32[8,384]{1,0:T(8,128)} %across.7) | copy-start | bytes 36868
  78.1 49.6 %collective-permute-start.10 = (f32[2,128,768]{2,1,0:T(8,128)}, f32[2,128,768]{2,1,0:T(8,128)}, u32[]{:S(2)}, u32[]{:S(2)}) collective-permute-start(f32[2,128,768]{2,1,0:T(8,128)} %broadcast_select_fusion.1), channel_id=1, source_target_pairs={{0,1},{1,0},{2,3},{3,2},{4,5},{5,4},{6,7},{7,6},{8,9},{9,8},{10,11... | collective-permute-start | bytes 2359304 | tf_op jit(solution)/shard_map/ppermute | solution.py:492
  82.0 45.7 %collective-permute-start.9 = (f32[2,128,768]{2,1,0:T(8,128)}, f32[2,128,768]{2,1,0:T(8,128)}, u32[]{:S(2)}, u32[]{:S(2)}) collective-permute-start(f32[2,128,768]{2,1,0:T(8,128)} %broadcast_select_fusion.2), channel_id=1, source_target_pairs={{0,1},{1,0},{2,3},{3,2},{4,5},{5,4},{6,7},{7,6},{8,9},{9,8},{10,11... | collective-permute-start | bytes 2359304 | tf_op jit(solution)/shard_map/ppermute | solution.py:492
  107.7 0.9 copy-start.1
  109.5 18.2 %collective-permute-start.11 = (f32[2,128,768]{2,1,0:T(8,128)}, f32[2,128,768]{2,1,0:T(8,128)S(1)}, u32[]{:S(2)}, u32[]{:S(2)}) collective-permute-start(f32[2,128,768]{2,1,0:T(8,128)} %broadcast_select_fusion), channel_id=1, source_target_pairs={{0,1},{1,0},{2,3},{3,2},{4,5},{5,4},{6,7},{7,6},{8,9},{9,8},{10,11... | collective-permute-start | bytes 2359304 | tf_op jit(solution)/shard_map/ppermute | solution.py:492
  115.0 32.4 %collective-permute-start.13 = (f32[1,384,384]{2,1,0:T(8,128)}, f32[1,384,384]{2,1,0:T(8,128)}, u32[]{:S(2)}, u32[]{:S(2)}) collective-permute-start(f32[1,384,384]{2,1,0:T(8,128)} %get-tuple-element.53), channel_id=1, source_target_pairs={{0,31},{1,2},{2,1},{3,4},{4,3},{5,6},{6,5},{7,8},{8,7},{9,10},{10,... | collective-permute-start | bytes 1769480 | tf_op jit(solution)/shard_map/ppermute | solution.py:492
  127.8 0.9 copy-start.4
  153.6 15.5 %collective-permute-start.15 = (f32[4,384,384]{2,1,0:T(8,128)}, f32[4,384,384]{2,1,0:T(8,128)}, u32[]{:S(2)}, u32[]{:S(2)}) collective-permute-start(f32[4,384,384]{2,1,0:T(8,128)} %get-tuple-element.59), channel_id=1, source_target_pairs={{0,1},{1,0},{2,3},{3,2},{4,5},{5,4},{6,7},{7,6},{8,9},{9,8},{10,11... | collective-permute-start | bytes 7077896 | tf_op jit(solution)/shard_map/ppermute | solution.py:492
  153.9 46.3 %collective-permute-start.17 = (f32[3,384,384]{2,1,0:T(8,128)}, f32[3,384,384]{2,1,0:T(8,128)}, u32[]{:S(2)}, u32[]{:S(2)}) collective-permute-start(f32[3,384,384]{2,1,0:T(8,128)} %get-tuple-element.62), channel_id=1, source_target_pairs={{0,31},{1,2},{2,1},{3,4},{4,3},{5,6},{6,5},{7,8},{8,7},{9,10},{10,... | collective-permute-start | bytes 5308424 | tf_op jit(solution)/shard_map/ppermute | solution.py:492
  155.9 57.2 %collective-permute-start.16 = (f32[1,384,384]{2,1,0:T(8,128)}, f32[1,384,384]{2,1,0:T(8,128)S(1)}, u32[]{:S(2)}, u32[]{:S(2)}) collective-permute-start(f32[1,384,384]{2,1,0:T(8,128)} %get-tuple-element.61), channel_id=1, source_target_pairs={{0,31},{1,2},{2,1},{3,4},{4,3},{5,6},{6,5},{7,8},{8,7},{9,10},{10,... | collective-permute-start | bytes 1769480 | tf_op jit(solution)/shard_map/ppermute | solution.py:492
  213.1 0.8 copy-start.5

commit v2 on v1

--- a/solution.py
+++ b/solution.py
@@ -18,7 +18,7 @@
 VMEM = pl.BlockSpec(memory_space=pltpu.VMEM)
 PARAMS = pltpu.CompilerParams(vmem_limit_bytes=63 * 1024 * 1024)
 
-INTRA, CROSS, ORDER, START, SEND_INTRA, SEND_CROSS, EARLY, EARLY_COUNT, LEFT, RIGHT, COLUMN, SECTIONS = range(12)
+CROSS, ORDER, START, SEND, EARLY, EARLY_COUNT, LEFT, RIGHT, COLUMN, SECTIONS = range(10)
 
 
 def after(value, *earlier):
@@ -54,13 +54,12 @@
     return wide[:, :nv] + wide[:, nv:] + dot_nt(hl, xh)
 
 
-def plan_kernel(devices, orbitals, where, couplings, lists_intra, lists_cross, pair_orbs, plan, seen):
+def plan_kernel(devices, orbitals, where, couplings, lists_cross, pair_orbs, plan, seen):
     pairs = couplings.shape[0]
     half = pairs // 2
     device = where[0]
     core = device % 2
     odd = (device // 2) % 2
-    partner = device + 1 - 2 * core
     outside = (device - 1 + 2 * core + devices) % devices
 
     def mark(lists, column, base):
@@ -103,10 +102,8 @@
         if cuts is not None:
             plan[cuts * pairs + keys] = filled
 
-    ranks(couplings, 1 - core, partner * pairs, INTRA)
     ranks(couplings, core, outside * pairs, CROSS)
-    sends(lists_intra, core, SEND_INTRA)
-    sends(lists_cross, 1 - core, SEND_CROSS)
+    sends(lists_cross, 1 - core, SEND)
     sort(ORDER, lambda p: plan[CROSS * pairs + p], half, START)
 
     swapped = (REACH + 1 - 2 * core) * orbitals
@@ -124,7 +121,6 @@
         late = late + seen[p]
     sort(EARLY, lambda p: seen[p], 2, None)
     plan[EARLY_COUNT * pairs] = pairs - late
-    plan[COLUMN * pairs] = 1 - core
     plan[COLUMN * pairs + 1] = core
     plan[COLUMN * pairs + 2] = swapped
     plan[COLUMN * pairs + 3] = near
@@ -132,27 +128,30 @@
     plan[COLUMN * pairs + 5] = 2 * REACH * orbitals - swapped
 
 
-def make_plan(devices, orbitals, where, couplings, lists_intra, lists_cross, pair_orbs):
+def make_plan(devices, orbitals, where, couplings, lists_cross, pair_orbs):
     pairs = couplings.shape[0]
     return pl.pallas_call(
         functools.partial(plan_kernel, devices, orbitals),
         out_shape=jax.ShapeDtypeStruct((SECTIONS * pairs,), jnp.int32),
-        in_specs=[SMEM] * 5,
+        in_specs=[SMEM] * 4,
         out_specs=SMEM,
         scratch_shapes=[pltpu.SMEM((pairs,), jnp.int32)],
         name="plan",
-    )(where, couplings, lists_intra, lists_cross, pair_orbs)
-
-
-def send_copies(p, plan, source, cross, intra, cross_sem, intra_sem, act):
+    )(where, couplings, lists_cross, pair_orbs)
+
+
+def send_copies(p, plan, source, outs, sem, act):
     pairs = plan.shape[0] // SECTIONS
-    for section, outs, sem in ((SEND_CROSS, cross, cross_sem), (SEND_INTRA, intra, intra_sem)):
-        place = plan[section * pairs + p]
-        for r, out in enumerate(outs):
-
-            @pl.when(place == r)
+    place = plan[SEND * pairs + p]
+    rank = 0
+    for out in outs:
+        for r in range(out.shape[0]):
+
+            @pl.when(place == rank)
             def _():
-                act(pltpu.make_async_copy(source, out, sem.at[r]))
+                act(pltpu.make_async_copy(source, out.at[r], sem.at[place]))
+
+            rank += 1
 
 
 def start(copy):
@@ -163,96 +162,91 @@
     copy.wait()
 
 
-def rank_groups(half):
-    return [(0, half - 1), (half - 1, half)]
-
-
-def send_shapes(half, nv):
-    sizes = [high - low for low, high in rank_groups(half)] + [half]
-    return [jax.ShapeDtypeStruct((size, nv, nv), f32) for size in sizes]
-
-
-def send_views(half, outs):
-    groups = rank_groups(half)
-    cross = [outs[k].at[r] for k, (low, high) in enumerate(groups) for r in range(high - low)]
-    return cross, [outs[len(groups)].at[r] for r in range(half)]
+def rank_groups(half, iteration):
+    cut = half // 2 if iteration == 0 else half - 1
+    return [(0, cut), (cut, half)]
+
+
+def send_shapes(half, nv, iteration):
+    return [jax.ShapeDtypeStruct((high - low, nv, nv), f32) for low, high in rank_groups(half, iteration)]
 
 
 def gather_kernel(plan, current, *rest):
-    outs, (rows, load_sem, cross_sem, intra_sem) = rest[:-4], rest[-4:]
+    outs, (rows, load_sem, send_sem) = rest[:-3], rest[-3:]
     pairs = current.shape[0]
-    half = pairs // 2
-    cross, intra = send_views(half, outs)
     loads = [pltpu.make_async_copy(current.at[p], rows.at[p], load_sem.at[p]) for p in range(pairs)]
-    for load in loads:
-        load.start()
+
+    def chosen(p, act):
+        @pl.when(plan[SEND * pairs + p] >= 0)
+        def _():
+            act(loads[p])
+
     for p in range(pairs):
-        loads[p].wait()
-        send_copies(p, plan, rows.at[p], cross, intra, cross_sem, intra_sem, start)
+        chosen(p, start)
     for p in range(pairs):
-        send_copies(p, plan, rows.at[p], cross, intra, cross_sem, intra_sem, wait)
+        chosen(p, wait)
+        send_copies(p, plan, rows.at[p], outs, send_sem, start)
+    for p in range(pairs):
+        send_copies(p, plan, rows.at[p], outs, send_sem, wait)
 
 
 def gather_rows(plan, current):
     pairs, nv, _ = current.shape
     half = pairs // 2
-    outs = pl.pallas_call(
+    shapes = send_shapes(half, nv, 0)
+    return pl.pallas_call(
         gather_kernel,
-        out_shape=send_shapes(half, nv),
+        out_shape=shapes,
         in_specs=[SMEM, ANY],
-        out_specs=[ANY] * len(send_shapes(half, nv)),
+        out_specs=[ANY] * len(shapes),
         scratch_shapes=[
             pltpu.VMEM((pairs, nv, nv), f32),
             pltpu.SemaphoreType.DMA((pairs,)),
             pltpu.SemaphoreType.DMA((half,)),
-            pltpu.SemaphoreType.DMA((half,)),
         ],
         compiler_params=PARAMS,
-        cost_estimate=cost(0, 2 * pairs * nv * nv * 4),
+        cost_estimate=cost(0, 2 * half * nv * nv * 4),
         name="gather_rows",
     )(plan, current)
-    return list(outs[:-1]), outs[-1]
-
-
-def couple_kernel(column, plan, x, t, gain, *rest):
-    p = pl.program_id(0)
-    c = column if column is not None else plan[COLUMN * pl.num_programs(0)]
-    value = project(x[0, 0], t[0], gain[p, c])
-    rest[-1][0] = value if len(rest) == 1 else rest[0][0] + value
-
-
-def couple(column, section, plan, x, t, gain, before=None):
+
+
+def couple_kernel(kind, low, pairs, adding, rows, x, t, gain, *rest):
+    p = low + pl.program_id(0)
+    value = project(x[0, 0], t[0], gain[p, rows[2 * pairs + kind]])
+    rest[-1][0] = rest[0][0] + value if adding else value
+
+
+def couple(kind, low, high, rows, x, t, gain, before=None, adding=False):
     pairs, _, nv, _ = x.shape
-    square = pl.BlockSpec((1, nv, nv), lambda p, plan: (p, 0, 0))
-    which = lambda plan: column if column is not None else plan[COLUMN * pairs]
+    square = pl.BlockSpec((1, nv, nv), lambda p, rows: (low + p, 0, 0))
     in_specs = [
-        pl.BlockSpec((1, 1, nv, nv), lambda p, plan: (p, which(plan), 0, 0)),
-        pl.BlockSpec((1, nv, nv), lambda p, plan: (plan[section * pairs + p], 0, 0)),
+        pl.BlockSpec((1, 1, nv, nv), lambda p, rows: (low + p, rows[2 * pairs + kind], 0, 0)),
+        pl.BlockSpec((1, nv, nv), lambda p, rows: (rows[kind * pairs + low + p], 0, 0)),
         SMEM,
     ]
     operands = [x, t, gain]
     if before is not None:
-        in_specs.append(square)
+        in_specs.append(square if adding else ANY)
         operands.append(before)
     return pl.pallas_call(
-        functools.partial(couple_kernel, column),
+        functools.partial(couple_kernel, kind, low, pairs, adding),
         out_shape=jax.ShapeDtypeStruct((pairs, nv, nv), f32),
         grid_spec=pltpu.PrefetchScalarGridSpec(
-            num_scalar_prefetch=1, grid=(pairs,), in_specs=in_specs, out_specs=square
+            num_scalar_prefetch=1, grid=(high - low,), in_specs=in_specs, out_specs=square
         ),
+        input_output_aliases={} if before is None else {4: 0},
         compiler_params=PARAMS,
-        cost_estimate=cost(pairs * 12 * nv**3, pairs * nv * nv * 12),
+        cost_estimate=cost((high - low) * 12 * nv**3, (high - low) * nv * nv * 12),
         name="couple",
-    )(plan, *operands)
+    )(rows, *operands)
 
 
 def finish_kernel(low, high, sending, plan, gain, occ, across, down, x, before, integral, own, *rest):
-    rest, scratch = rest[:-12], rest[-12:]
-    x_buf, t_buf, before_buf, integral_buf, own_buf, out_buf, sem, t_sem, out_sem, cross_sem, intra_sem, _ = scratch
+    rest, scratch = rest[:-10], rest[-10:]
+    x_buf, t_buf, before_buf, integral_buf, own_buf, out_buf, sem, t_sem, out_sem, send_sem = scratch
     pairs = x.shape[0]
-    half = pairs // 2
     t = rest[0]
-    outs = rest[len(rest) - (len(rank_groups(half)) + 2 if sending else 1) :]
+    outs = rest[len(rest) - (3 if sending else 1) :]
     out = outs[0]
     first = plan[START * pairs + low]
     count = plan[START * pairs + high] - first
@@ -272,8 +266,7 @@
         p = pair(s)
         act(pltpu.make_async_copy(out_buf.at[s], out.at[p], out_sem.at[s]))
         if sending:
-            cross, intra = send_views(half, outs[1:])
-            send_copies(p, plan, out_buf.at[s], cross, intra, cross_sem, intra_sem, act)
+            send_copies(p, plan, out_buf.at[s], outs[1:], send_sem, act)
 
     t_copies = [pltpu.make_async_copy(t.at[k], t_buf.at[k], t_sem.at[k]) for k in range(high - low)]
 
@@ -325,7 +318,7 @@
     in_specs = [SMEM] * 3 + [VMEM] * 2 + [ANY] * 5
     out_shape = [jax.ShapeDtypeStruct((pairs, nv, nv), f32)]
     if sending:
-        out_shape += send_shapes(half, nv)
+        out_shape += send_shapes(half, nv, 1)
     aliases = {}
     if done is not None:
         aliases = {len(operands) + k: k for k in range(len(done))}
@@ -348,8 +341,6 @@
             pltpu.SemaphoreType.DMA((high - low,)),
             pltpu.SemaphoreType.DMA((pairs,)),
             pltpu.SemaphoreType.DMA((half,)),
-            pltpu.SemaphoreType.DMA((half,)),
-            pltpu.SMEM((1,), jnp.int32),
         ],
         input_output_aliases=aliases,
         compiler_params=PARAMS,
@@ -358,42 +349,34 @@
     )(*operands)
 
 
-def integrals_kernel(early, wholes, pieces, plan, slabs, *rest):
+def integrals_kernel(early, groups, plan, slabs, *rest):
     rest, (left_buf, high, low, right_buf, out_buf, left_sem, right_sem, out_sem) = rest[:-8], rest[-8:]
     out = rest[-1]
     orbitals, nv, nq = slabs.shape
     pairs = out.shape[0]
-    per = pieces
-    rows = nv // per
-    bases = plan[COLUMN * pairs + 2], plan[COLUMN * pairs + 3], plan[COLUMN * pairs + 4], plan[COLUMN * pairs + 5]
-    sources = []
-    if wholes:
-        whole = rest[0]
-        sources.append((bases[0], [[whole.at[o, pl.ds(k * rows, rows)] for k in range(per)] for o in range(orbitals)]))
-    used = wholes
-    for base in ((bases[1],) if early else (bases[2], bases[3])):
-        refs = rest[used : used + pieces]
+    sources, used = [], 0
+    for k, pieces in enumerate(groups):
+        sources.append((plan[COLUMN * pairs + (2 if early else 4) + k], rest[used : used + pieces]))
         used += pieces
-        sources.append((base, [[refs[k].at[o] for k in range(per)] for o in range(orbitals)]))
     count = plan[EARLY_COUNT * pairs] if early else pairs - plan[EARLY_COUNT * pairs]
     first = 0 if early else plan[EARLY_COUNT * pairs]
     pair = lambda s: plan[EARLY * pairs + first + s]
 
     def fetch(s, slot):
         right = plan[RIGHT * pairs + pair(s)]
-        for base, held in sources:
+        for base, pieces in sources:
             for o in range(orbitals):
 
                 @pl.when(right == base + o)
                 def _():
-                    for k in range(per):
-                        target = right_buf.at[slot, pl.ds(k * rows, rows)]
-                        pltpu.make_async_copy(held[o][k], target, right_sem.at[slot, k]).start()
+                    at = 0
+                    for piece in pieces:
+                        target = right_buf.at[slot, pl.ds(at, piece.shape[1])]
+                        pltpu.make_async_copy(piece.at[o], target, right_sem.at[slot]).start()
+                        at += piece.shape[1]
 
     def arrived(slot):
-        for k in range(per):
-            target = right_buf.at[slot, pl.ds(k * rows, rows)]
-            pltpu.make_async_copy(slabs.at[0, pl.ds(k * rows, rows)], target, right_sem.at[slot, k]).wait()
+        pltpu.make_async_copy(slabs.at[0], right_buf.at[slot], right_sem.at[slot]).wait()
 
     def store(s, slot):
         return pltpu.make_async_copy(out_buf.at[slot], out.at[pair(s)], out_sem.at[slot])
@@ -441,10 +424,10 @@
         store(count - 1, (count + 1) % 2).wait()
 
 
-def pair_integrals(early, plan, slabs, pairs, wholes, pieces, done=None):
+def pair_integrals(early, plan, slabs, pairs, groups, done=None):
     orbitals, nv, nq = slabs.shape
-    operands = [plan, slabs, *wholes]
-    for group in pieces:
+    operands = [plan, slabs]
+    for group in groups:
         operands += group
     in_specs = [SMEM] + [ANY] * (len(operands) - 1)
     aliases = {}
@@ -453,7 +436,7 @@
         operands.append(done)
         in_specs.append(ANY)
     return pl.pallas_call(
-        functools.partial(integrals_kernel, early, len(wholes), len(pieces[0])),
+        functools.partial(integrals_kernel, early, [len(group) for group in groups]),
         out_shape=jax.ShapeDtypeStruct((pairs, nv, nv), f32),
         in_specs=in_specs,
         out_specs=ANY,
@@ -464,7 +447,7 @@
             pltpu.VMEM((2, nv, nq), f32),
             pltpu.VMEM((2, nv, nv), f32),
             pltpu.SemaphoreType.DMA((orbitals,)),
-            pltpu.SemaphoreType.DMA((2, len(pieces[0]))),
+            pltpu.SemaphoreType.DMA((2,)),
             pltpu.SemaphoreType.DMA((2,)),
         ],
         input_output_aliases=aliases,
@@ -491,45 +474,50 @@
     far_perm = [(i, (i - 4 if chip_odd(i) else i + 4) % count) for i in everyone]
     send = lambda value, perm: lax.ppermute(value, axis, perm)
 
-    lists_intra = send(couplings, inside)
     lists_cross = send(couplings, beside)
     rows = nv // CHUNKS
     pieces = [slabs[:, k * rows : (k + 1) * rows] for k in range(CHUNKS)]
-    *pieces, lists_intra, lists_cross = lax.optimization_barrier((*pieces, lists_intra, lists_cross))
+    *pieces, lists_cross = lax.optimization_barrier((*pieces, lists_cross))
     near = [send(piece, near_perm) for piece in pieces]
-
-    own_row = couplings[:, 2] - device * pairs
-    partial = couple(2, 0, after(own_row, *pieces), intersections, amplitudes, fock_coupling)
+    intra_t = send(amplitudes, inside)
+    slabs_swapped = send(slabs, inside)
+
+    core = device % 2
+    partner = device + 1 - 2 * core
+    intra_list = jnp.where(core == 0, couplings[:, 1], couplings[:, 0])
+    coupled_rows = jnp.concatenate(
+        [couplings[:, 2] - device * pairs, intra_list - partner * pairs, jnp.stack([2 + 0 * core, 1 - core])]
+    )
+
+    partial = couple(0, 0, pairs, after(coupled_rows, *pieces), intersections, amplitudes, fock_coupling)
     near[0], partial = lax.optimization_barrier((near[0], partial))
     far = [send(near[0], far_perm)]
-
-    where = after(device.astype(jnp.int32).reshape(1), partial)
-    plan = make_plan(count, orbitals, where, couplings, lists_intra, lists_cross, pair_orbs)
+    partial = couple(1, 0, pairs, coupled_rows, intersections, intra_t, fock_coupling, partial, True)
+    near[1], partial = lax.optimization_barrier((near[1], partial))
+    far.append(send(near[1], far_perm))
+
+    where = after(device.astype(jnp.int32).reshape(1), near[1])
+    plan = make_plan(count, orbitals, where, couplings, lists_cross, pair_orbs)
     across, down = virt_energy, virt_energy.T
-    cross_out, intra_out = gather_rows(plan, amplitudes)
-    intra_t = send(intra_out, inside)
-    slabs_swapped = send(after(slabs, intra_out), inside)
-
-    near[1], intra_out = lax.optimization_barrier((near[1], intra_out))
-    far.append(send(near[1], far_perm))
-    partial = couple(None, INTRA, plan, intersections, intra_t, fock_coupling, after(partial, near[1]))
-    near[2], far[0], partial, *cross_out = lax.optimization_barrier((near[2], far[0], partial, *cross_out))
+    cross_out = gather_rows(plan, amplitudes)
     cross_t = [send(rows_out, beside) for rows_out in cross_out]
+    near[2], far[0], plan, *_ = lax.optimization_barrier((near[2], far[0], plan, *cross_out))
     far.append(send(near[2], far_perm))
+    integrals = pair_integrals(True, plan, slabs, pairs, [[slabs_swapped], near])
+    far[2], integrals = lax.optimization_barrier((far[2], integrals))
     relayed = [send(jnp.where(selects_near, n, f), inside) for n, f in zip(near, far)]
-    integrals = pair_integrals(True, plan, after(slabs, partial), pairs, [slabs_swapped], [near])
-    integrals = pair_integrals(False, plan, slabs, pairs, [], [far, relayed], integrals)
+    integrals = pair_integrals(False, plan, slabs, pairs, [far, relayed], integrals)
 
     current = amplitudes
     for iteration in range(ITERS):
         if iteration > 0:
             cross_t = [send(rows_out, beside) for rows_out in cross_out]
-            intra_t = send(intra_out, inside)
-            partial = couple(2, 0, own_row, intersections, current, fock_coupling)
-            partial = couple(None, INTRA, plan, intersections, intra_t, fock_coupling, partial)
+            intra_t = send(current, inside)
+            partial = couple(0, 0, pairs, coupled_rows, intersections, current, fock_coupling)
+            partial = couple(1, 0, pairs, coupled_rows, intersections, intra_t, fock_coupling, partial, True)
         sending = iteration + 1 < ITERS
         done = None
-        for k, (low, high) in enumerate(rank_groups(half)):
+        for k, (low, high) in enumerate(rank_groups(half, iteration)):
             done = finish(
                 low,
                 high,
@@ -548,7 +536,7 @@
             )
         current = done[0]
         if sending:
-            cross_out, intra_out = done[1:-1], done[-1]
+            cross_out = done[1:]
     return current
 
 

time: 222 us -> 201 us (0.905)
  the two profiles are of different devices: /device:TPU:1 before, /device:TPU:5 now
where the time goes in v2:
time: 201 us; the launch traced here: 199 us
  Pallas kernels  113 us (56%)
  waiting for transfers between devices  51.6 us (26%)
  starting transfers between devices  23.5 us (12%)
  local copies, waits for them, and re-layouts  6.71 us (3%)
  other arithmetic  4.09 us (2%)
    pallas_call x4, Pallas kernels, couple(): pl.pallas_call(functools.partial(couple_kernel, kind, low, pairs, adding)...  53.9 us
    ppermute x17, waiting for transfers between devices, shards(): send = lambda value, perm: lax.ppermute(value, axis, perm)  51.6 us
    pallas_call x4, Pallas kernels, finish(): pl.pallas_call(functools.partial(finish_kernel, low, high, sending), out_...  38.3 us
    ppermute x17, starting transfers between devices, shards(): send = lambda value, perm: lax.ppermute(value, axis, perm)  23.5 us
    pallas_call x2, Pallas kernels, pair_integrals(): pl.pallas_call(functools.partial(integrals_kernel, early, [len(group) for...  16.2 us
  transfers between devices with their start and end apart: 17, of which 6 were waited for; matrix products, arithmetic and copies ran while one was open for 5% of the time, Pallas kernels for 49%

profile of v2, /device:TPU:5, one launch (start us, length us, event | category | flops | bytes accessed | tf_op | source)
XLA Modules:
  0.0 199.3 jit_solution(3884005858176495036)
XLA Ops:
  0.0 0.7 collective-permute-start.5
  0.7 0.8 copy.16.couplings
  1.4 1.2 collective-permute-start
  2.6 0.4 collective-permute-start.8
  3.0 3.0 %fusion.2 = (f32[2,128,768]{2,1,0:T(8,128)}, f32[2,128,768]{2,1,0:T(8,128)}, f32[2,128,768]{2,1,0:T(8,128)S(1)}) fusion(f32[2,384,768]{2,1,0:T(8,128)} %slabs.3), kind=kLoop, calls=%fused_computation.8 | loop fusion | bytes 4718592 | tf_op jit(solution)/shard_map/slice | solution.py:479
  6.0 1.5 collective-permute-start.2
  7.5 0.7 copy.17.gain
  8.2 0.0 collective-permute-start.4
  8.2 0.6 pad_add_fusion.rows
  8.8 1.5 collective-permute-start.1
  10.3 13.1 %couple.4.rest_0_ = f32[8,384,384]{2,1,0:T(8,128)} custom-call(s32[18]{0:T(128)} %pad_add_fusion.rows, f32[8,3,384,384]{3,2,1,0:T(8,128)} %x.15, f32[8,384,384]{2,1,0:T(8,128)} %own.3, f32[8,3]{1,0:T(8,128)} %copy.17.gain), custom_call_target="tpu_custom_call" | custom-call | flops 5435817 | bytes 14155 | tf_op jit(solution)/shard_map/couple/pallas_call | solution.py:231
  23.4 0.0 copy-start.8
  23.4 1.8 collective-permute-done.2.rest_1_
  25.2 2.2 %collective-permute-start.3 = (f32[2,128,768]{2,1,0:T(8,128)}, f32[2,128,768]{2,1,0:T(8,128)S(1)}, u32[]{:S(2)}, u32[]{:S(2)}) collective-permute-start(f32[2,128,768]{2,1,0:T(8,128)} %collective-permute-done.2.rest_1_), channel_id=1, source_target_pairs={{0,4},{1,5},{2,30},{3,31},{4,8},{5,9},{6,2},{7,3},{8,12},{9,13},{1... | collective-permute-start | bytes 2359304 | tf_op jit(solution)/shard_map/ppermute | solution.py:475
  27.4 0.0 collective-permute-done.5.t
  27.4 13.8 %couple.5.before = f32[8,384,384]{2,1,0:T(8,128)} custom-call(s32[18]{0:T(128)} %pad_add_fusion.rows, f32[8,3,384,384]{3,2,1,0:T(8,128)} %x.15, f32[8,384,384]{2,1,0:T(8,128)} %collective-permute-done.5.t, f32[8,3]{1,0:T(8,128)} %copy.17.gain, f32[8,384,384]{2,1,0:T(8,128)} %couple.4.rest_0_), custom_call_target="tpu_custom_call", output_to_operand_aliasing={{}: (4, {})} | custom-call | flops 5435817 | bytes 14155 | tf_op jit(solution)/shard_map/couple/pallas_call | solution.py:231
  41.2 0.8 collective-permute-done.4.rest_2_
  42.1 2.2 %collective-permute-start.6 = (f32[2,128,768]{2,1,0:T(8,128)}, f32[2,128,768]{2,1,0:T(8,128)}, u32[]{:S(2)}, u32[]{:S(2)}) collective-permute-start(f32[2,128,768]{2,1,0:T(8,128)} %collective-permute-done.4.rest_2_), channel_id=1, source_target_pairs={{0,4},{1,5},{2,30},{3,31},{4,8},{5,9},{6,2},{7,3},{8,12},{9,13},{1... | collective-permute-start | bytes 2359304 | tf_op jit(solution)/shard_map/ppermute | solution.py:475
  44.2 0.7 copy.20.pair_orbs
  44.9 1.6 plan.1
  46.5 3.3 %gather_rows.1 = (f32[2,384,384]{2,1,0:T(8,128)}, f32[2,384,384]{2,1,0:T(8,128)}) custom-call(s32[72]{0:T(128)} %plan.1, f32[8,384,384]{2,1,0:T(8,128)} %own.3), custom_call_target="tpu_custom_call" | custom-call | bytes 4718 | tf_op jit(solution)/shard_map/gather_rows/pallas_call | solution.py:197
  49.9 9.0 %collective-permute-done.1.rest_3_ = f32[2,128,768]{2,1,0:T(8,128)} collective-permute-done((f32[2,128,768]{2,1,0:T(8,128)}, f32[2,128,768]{2,1,0:T(8,128)}, u32[]{:S(2)}, u32[]{:S(2)}) %collective-permute-start.1) | collective-permute-done | bytes 786464 | tf_op jit(solution)/shard_map/ppermute | solution.py:475
  58.9 2.2 %collective-permute-start.7 = (f32[2,128,768]{2,1,0:T(8,128)}, f32[2,128,768]{2,1,0:T(8,128)}, u32[]{:S(2)}, u32[]{:S(2)}) collective-permute-start(f32[2,128,768]{2,1,0:T(8,128)} %collective-permute-done.1.rest_3_), channel_id=1, source_target_pairs={{0,4},{1,5},{2,30},{3,31},{4,8},{5,9},{6,2},{7,3},{8,12},{9,13},{1... | collective-permute-start | bytes 2359304 | tf_op jit(solution)/shard_map/ppermute | solution.py:475
  61.1 3.1 %collective-permute-start.13 = (f32[2,384,384]{2,1,0:T(8,128)}, f32[2,384,384]{2,1,0:T(8,128)}, u32[]{:S(2)}, u32[]{:S(2)}) collective-permute-start(f32[2,384,384]{2,1,0:T(8,128)} %get-tuple-element.37), channel_id=1, source_target_pairs={{0,31},{1,2},{2,1},{3,4},{4,3},{5,6},{6,5},{7,8},{8,7},{9,10},{10,... | collective-permute-start | bytes 3538952 | tf_op jit(solution)/shard_map/ppermute | solution.py:475
  64.2 0.0 collective-permute-start.12
  64.2 1.0 broadcast_select_fusion.2
  65.2 1.7 collective-permute-start.9
  66.9 5.6 %pair_integrals.2.rest_6_ = f32[8,384,384]{2,1,0:T(8,128)} custom-call(s32[72]{0:T(128)} %plan.1, f32[2,384,768]{2,1,0:T(8,128)} %slabs.3, f32[2,384,768]{2,1,0:T(8,128)} %collective-permute-done.8.rest_0_, f32[2,128,768]{2,1,0:T(8,128)} %collective-permute-done.2.rest_1_, f32[2,128,768]{2,1,0:T(8,128)} %collective-permute-done.4.rest_2_, ...), custom_call_target="tpu_custom_call" | custom-call | flops 2717908 | bytes 4718 | tf_op jit(solution)/shard_map/pair_integrals/pallas_call | solution.py:438
  72.6 0.0 copy-start.3
  72.6 1.2 broadcast_select_fusion.1
  73.8 2.6 %collective-permute-start.10 = (f32[2,128,768]{2,1,0:T(8,128)S(1)}, f32[2,128,768]{2,1,0:T(8,128)S(1)}, u32[]{:S(2)}, u32[]{:S(2)}) collective-permute-start(f32[2,128,768]{2,1,0:T(8,128)S(1)} %broadcast_select_fusion.1), channel_id=1, source_target_pairs={{0,1},{1,0},{2,3},{3,2},{4,5},{5,4},{6,7},{7,6},{8,9},{9,8},{10,11... | collective-permute-start | bytes 2359304 | tf_op jit(solution)/shard_map/ppermute | solution.py:475
  76.5 19.6 %collective-permute-done.7.rest_2_ = f32[2,128,768]{2,1,0:T(8,128)} collective-permute-done((f32[2,128,768]{2,1,0:T(8,128)}, f32[2,128,768]{2,1,0:T(8,128)}, u32[]{:S(2)}, u32[]{:S(2)}) %collective-permute-start.7) | collective-permute-done | bytes 786464 | tf_op jit(solution)/shard_map/ppermute | solution.py:475
  96.0 1.2 broadcast_select_fusion
  97.3 2.4 %collective-permute-start.11 = (f32[2,128,768]{2,1,0:T(8,128)S(1)}, f32[2,128,768]{2,1,0:T(8,128)}, u32[]{:S(2)}, u32[]{:S(2)}) collective-permute-start(f32[2,128,768]{2,1,0:T(8,128)S(1)} %broadcast_select_fusion), channel_id=1, source_target_pairs={{0,1},{1,0},{2,3},{3,2},{4,5},{5,4},{6,7},{7,6},{8,9},{9,8},{10,11... | collective-permute-start | bytes 2359304 | tf_op jit(solution)/shard_map/ppermute | solution.py:475
  99.7 0.8 copy.21
  100.5 1.2 collective-permute-done.11.rest_5_
  101.7 10.6 %pair_integrals.3.integral = f32[8,384,384]{2,1,0:T(8,128)} custom-call(s32[72]{0:T(128)} %plan.1, f32[2,384,768]{2,1,0:T(8,128)} %slabs.3, f32[2,128,768]{2,1,0:T(8,128)} %copy-done, f32[2,128,768]{2,1,0:T(8,128)} %collective-permute-done.6.rest_1_, f32[2,128,768]{2,1,0:T(8,128)} %collective-permute-done.7.rest_2_, ...), custom_call_target="tpu_custom_call", output_to_operand_aliasing={{}: (8, {})} | custom-call | flops 2717908 | bytes 4718 | tf_op jit(solution)/shard_map/pair_integrals/pallas_call | solution.py:438
  112.3 9.7 %finish.4 = (f32[8,384,384]{2,1,0:T(8,128)}, f32[3,384,384]{2,1,0:T(8,128)}, f32[1,384,384]{2,1,0:T(8,128)}) custom-call(s32[72]{0:T(128)} %plan.1, f32[8,3]{1,0:T(8,128)} %copy.17.gain, f32[8]{0:T(128)} %occ.7, f32[8,384]{1,0:T(8,128)} %across.7, f32[384,8]{1,0:T(8,128)} %bitcast.7, f32[8,3,384,384]{3,2,1,0:T(8,128)} %x.15, f32[8,384,384]{2,1,0:T(8,128)} %couple.5.before, ...), custom_call_target="tpu_custom_call" | custom-call | flops 2717908 | bytes 14155 | tf_op jit(solution)/shard_map/finish/pallas_call | solution.py:328
  122.0 9.7 %finish.5 = (f32[8,384,384]{2,1,0:T(8,128)}, f32[3,384,384]{2,1,0:T(8,128)}, f32[1,384,384]{2,1,0:T(8,128)}) custom-call(s32[72]{0:T(128)} %plan.1, f32[8,3]{1,0:T(8,128)} %copy.17.gain, f32[8]{0:T(128)} %occ.7, f32[8,384]{1,0:T(8,128)} %across.7, f32[384,8]{1,0:T(8,128)} %bitcast.8, ...), custom_call_target="tpu_custom_call", output_to_operand_aliasing={{0}: (10, {}), {1}: (11, {}), {2}: (12, {})} | custom-call | flops 2717908 | bytes 14155 | tf_op jit(solution)/shard_map/finish/pallas_call | solution.py:328
  131.7 0.1 collective-permute-start.14
  131.8 0.1 collective-permute-start.16
  131.9 1.7 collective-permute-start.15
  133.6 13.1 %couple.6.rest_0_ = f32[8,384,384]{2,1,0:T(8,128)} custom-call(s32[18]{0:T(128)} %pad_add_fusion.rows, f32[8,3,384,384]{3,2,1,0:T(8,128)} %x.15, f32[8,384,384]{2,1,0:T(8,128)} %get-tuple-element.48.t.own, f32[8,3]{1,0:T(8,128)} %copy.17.gain), custom_call_target="tpu_custom_call" | custom-call | flops 5435817 | bytes 14155 | tf_op jit(solution)/shard_map/couple/pallas_call | solution.py:231
  146.7 13.8 %couple.7.before = f32[8,384,384]{2,1,0:T(8,128)} custom-call(s32[18]{0:T(128)} %pad_add_fusion.rows, f32[8,3,384,384]{3,2,1,0:T(8,128)} %x.15, f32[8,384,384]{2,1,0:T(8,128)} %collective-permute-done.14.t, f32[8,3]{1,0:T(8,128)} %copy.17.gain, f32[8,384,384]{2,1,0:T(8,128)} %couple.6.rest_0_), custom_call_target="tpu_custom_call", output_to_operand_aliasing={{}: (4, {})} | custom-call | flops 5435817 | bytes 14155 | tf_op jit(solution)/shard_map/couple/pallas_call | solution.py:231
  160.5 19.0 %collective-permute-done.16.rest_0_ = f32[3,384,384]{2,1,0:T(8,128)} collective-permute-done((f32[3,384,384]{2,1,0:T(8,128)}, f32[3,384,384]{2,1,0:T(8,128)}, u32[]{:S(2)}, u32[]{:S(2)}) %collective-permute-start.16) | collective-permute-done | bytes 1769504 | tf_op jit(solution)/shard_map/ppermute | solution.py:475
  179.6 12.8 %finish.6.rest_1_ = f32[8,384,384]{2,1,0:T(8,128)} custom-call(s32[72]{0:T(128)} %plan.1, f32[8,3]{1,0:T(8,128)} %copy.17.gain, f32[8]{0:T(128)} %occ.7, f32[8,384]{1,0:T(8,128)} %across.7, f32[384,8]{1,0:T(8,128)} %bitcast.9, f32[8,3,384,384]{3,2,1,0:T(8,128)} %x.15, f32[8,384,384]{2,1,0:T(8,128)} %couple.7.before, f32[8,384,384]{2,1,0:T(8,128)} %pair_integrals.3.integral, ...), custom_call_target="tpu_custom_call" | custom-call | flops 4076863 | bytes 21233 | tf_op jit(solution)/shard_map/finish/pallas_call | solution.py:328
  192.4 0.8 copy-done.2
  193.2 6.1 %finish.7 = f32[8,384,384]{2,1,0:T(8,128)} custom-call(s32[72]{0:T(128)} %plan.1, f32[8,3]{1,0:T(8,128)} %copy.17.gain, f32[8]{0:T(128)} %occ.7, f32[8,384]{1,0:T(8,128)} %across.7, f32[384,8]{1,0:T(8,128)} %bitcast.10, f32[8,3,384,384]{3,2,1,0:T(8,128)} %x.15, f32[8,384,384]{2,1,0:T(8,128)} %couple.7.before, ...), custom_call_target="tpu_custom_call", output_to_operand_aliasing={{}: (10, {})} | custom-call | flops 1358954 | bytes 7077 | tf_op jit(solution)/shard_map/finish/pallas_call | solution.py:328
  (26 shorter events, 0.1 us)
Async XLA Ops:
  0.0 8.2 %copy-start.5 = (s32[8,3]{0,1:T(4,128)S(1)}, s32[8,3]{0,1:T(4,128)}, u32[]{:S(2)}) copy-start(s32[8,3]{0,1:T(4,128)} %param.15) | copy-start | bytes 292
  0.0 7.5 %copy-start.7 = (f32[8,3]{0,1:T(4,128)S(1)}, f32[8,3]{0,1:T(4,128)}, u32[]{:S(2)}) copy-start(f32[8,3]{0,1:T(4,128)} %param.11) | copy-start | bytes 292
  0.0 27.4 %collective-permute-start.5 = (f32[8,384,384]{2,1,0:T(8,128)}, f32[8,384,384]{2,1,0:T(8,128)}, u32[]{:S(2)}, u32[]{:S(2)}) collective-permute-start(f32[8,384,384]{2,1,0:T(8,128)} %own.3), channel_id=1, source_target_pairs={{0,1},{1,0},{2,3},{3,2},{4,5},{5,4},{6,7},{7,6},{8,9},{9,8},{10,11... | collective-permute-start | bytes 14155784 | tf_op jit(solution)/shard_map/ppermute | solution.py:475
  1.4 21.9 %copy-start.4 = (s32[8,3]{1,0:T(8,128)}, s32[8,3]{1,0:T(8,128)S(1)}, u32[]{:S(2)}) copy-start(s32[8,3]{1,0:T(8,128)S(1)} %copy.16.couplings) | copy-start | bytes 292
  1.4 4.5 %collective-permute-start = (s32[8,3]{1,0:T(8,128)S(1)}, s32[8,3]{1,0:T(8,128)S(1)}, u32[]{:S(2)}, u32[]{:S(2)}) collective-permute-start(s32[8,3]{1,0:T(8,128)S(1)} %copy.16.couplings), channel_id=1, source_target_pairs={{0,31},{1,2},{2,1},{3,4},{4,3},{5,6},{6,5},{7,8},{8,7},{9,10},{10,... | collective-permute-start | bytes 296 | tf_op jit(solution)/shard_map/ppermute | solution.py:475
  2.6 62.6 %collective-permute-start.8 = (f32[2,384,768]{2,1,0:T(8,128)}, f32[2,384,768]{2,1,0:T(8,128)}, u32[]{:S(2)}, u32[]{:S(2)}) collective-permute-start(f32[2,384,768]{2,1,0:T(8,128)} %slabs.3), channel_id=1, source_target_pairs={{0,1},{1,0},{2,3},{3,2},{4,5},{5,4},{6,7},{7,6},{8,9},{9,8},{10,11... | collective-permute-start | bytes 7077896 | tf_op jit(solution)/shard_map/ppermute | solution.py:475
  6.0 17.4 %copy-start.6 = (s32[8,3]{1,0:T(8,128)}, s32[8,3]{1,0:T(8,128)S(1)}, u32[]{:S(2)}) copy-start(s32[8,3]{1,0:T(8,128)S(1)} %collective-permute-done.lists_cross) | copy-start | bytes 292
  6.0 19.2 %collective-permute-start.2 = (f32[2,128,768]{2,1,0:T(8,128)S(1)}, f32[2,128,768]{2,1,0:T(8,128)}, u32[]{:S(2)}, u32[]{:S(2)}) collective-permute-start(f32[2,128,768]{2,1,0:T(8,128)S(1)} %get-tuple-element.29), channel_id=1, source_target_pairs={{0,2},{1,3},{2,0},{3,1},{4,6},{5,7},{6,4},{7,5},{8,10},{9,11},{10,... | collective-permute-start | bytes 2359304 | tf_op jit(solution)/shard_map/ppermute | solution.py:475
  8.2 33.9 %collective-permute-start.4 = (f32[2,128,768]{2,1,0:T(8,128)}, f32[2,128,768]{2,1,0:T(8,128)}, u32[]{:S(2)}, u32[]{:S(2)}) collective-permute-start(f32[2,128,768]{2,1,0:T(8,128)} %get-tuple-element.30), channel_id=1, source_target_pairs={{0,2},{1,3},{2,0},{3,1},{4,6},{5,7},{6,4},{7,5},{8,10},{9,11},{10,... | collective-permute-start | bytes 2359304 | tf_op jit(solution)/shard_map/ppermute | solution.py:475
  8.8 50.1 %collective-permute-start.1 = (f32[2,128,768]{2,1,0:T(8,128)}, f32[2,128,768]{2,1,0:T(8,128)}, u32[]{:S(2)}, u32[]{:S(2)}) collective-permute-start(f32[2,128,768]{2,1,0:T(8,128)} %get-tuple-element.28), channel_id=1, source_target_pairs={{0,2},{1,3},{2,0},{3,1},{4,6},{5,7},{6,4},{7,5},{8,10},{9,11},{10,... | collective-permute-start | bytes 2359304 | tf_op jit(solution)/shard_map/ppermute | solution.py:475
  23.4 20.8 %copy-start.8 = (s32[8,2]{0,1:T(2,128)S(1)}, s32[8,2]{0,1:T(2,128)}, u32[]{:S(2)}) copy-start(s32[8,2]{0,1:T(2,128)} %param.14) | copy-start | bytes 196
  25.2 33.7 %collective-permute-start.3 = (f32[2,128,768]{2,1,0:T(8,128)}, f32[2,128,768]{2,1,0:T(8,128)S(1)}, u32[]{:S(2)}, u32[]{:S(2)}) collective-permute-start(f32[2,128,768]{2,1,0:T(8,128)} %collective-permute-done.2.rest_1_), channel_id=1, source_target_pairs={{0,4},{1,5},{2,30},{3,31},{4,8},{5,9},{6,2},{7,3},{8,12},{9,13},{1... | collective-permute-start | bytes 2359304 | tf_op jit(solution)/shard_map/ppermute | solution.py:475
  42.1 30.5 %collective-permute-start.6 = (f32[2,128,768]{2,1,0:T(8,128)}, f32[2,128,768]{2,1,0:T(8,128)}, u32[]{:S(2)}, u32[]{:S(2)}) collective-permute-start(f32[2,128,768]{2,1,0:T(8,128)} %collective-permute-done.4.rest_2_), channel_id=1, source_target_pairs={{0,4},{1,5},{2,30},{3,31},{4,8},{5,9},{6,2},{7,3},{8,12},{9,13},{1... | collective-permute-start | bytes 2359304 | tf_op jit(solution)/shard_map/ppermute | solution.py:475
  58.9 13.7 %copy-start = (f32[2,128,768]{2,1,0:T(8,128)}, f32[2,128,768]{2,1,0:T(8,128)S(1)}, u32[]{:S(2)}) copy-start(f32[2,128,768]{2,1,0:T(8,128)S(1)} %collective-permute-done.3.rest_0_) | copy-start | bytes 2359300
  58.9 37.1 %collective-permute-start.7 = (f32[2,128,768]{2,1,0:T(8,128)}, f32[2,128,768]{2,1,0:T(8,128)}, u32[]{:S(2)}, u32[]{:S(2)}) collective-permute-start(f32[2,128,768]{2,1,0:T(8,128)} %collective-permute-done.1.rest_3_), channel_id=1, source_target_pairs={{0,4},{1,5},{2,30},{3,31},{4,8},{5,9},{6,2},{7,3},{8,12},{9,13},{1... | collective-permute-start | bytes 2359304 | tf_op jit(solution)/shard_map/ppermute | solution.py:475
  61.1 51.2 %collective-permute-start.13 = (f32[2,384,384]{2,1,0:T(8,128)}, f32[2,384,384]{2,1,0:T(8,128)}, u32[]{:S(2)}, u32[]{:S(2)}) collective-permute-start(f32[2,384,384]{2,1,0:T(8,128)} %get-tuple-element.37), channel_id=1, source_target_pairs={{0,31},{1,2},{2,1},{3,4},{4,3},{5,6},{6,5},{7,8},{8,7},{9,10},{10,... | collective-permute-start | bytes 3538952 | tf_op jit(solution)/shard_map/ppermute | solution.py:475
  64.2 57.8 %collective-permute-start.12 = (f32[2,384,384]{2,1,0:T(8,128)}, f32[2,384,384]{2,1,0:T(8,128)}, u32[]{:S(2)}, u32[]{:S(2)}) collective-permute-start(f32[2,384,384]{2,1,0:T(8,128)} %get-tuple-element.38), channel_id=1, source_target_pairs={{0,31},{1,2},{2,1},{3,4},{4,3},{5,6},{6,5},{7,8},{8,7},{9,10},{10,... | collective-permute-start | bytes 3538952 | tf_op jit(solution)/shard_map/ppermute | solution.py:475
  65.2 35.3 %collective-permute-start.9 = (f32[2,128,768]{2,1,0:T(8,128)}, f32[2,128,768]{2,1,0:T(8,128)}, u32[]{:S(2)}, u32[]{:S(2)}) collective-permute-start(f32[2,128,768]{2,1,0:T(8,128)} %broadcast_select_fusion.2), channel_id=1, source_target_pairs={{0,1},{1,0},{2,3},{3,2},{4,5},{5,4},{6,7},{7,6},{8,9},{9,8},{10,11... | collective-permute-start | bytes 2359304 | tf_op jit(solution)/shard_map/ppermute | solution.py:475
  72.6 27.1 %copy-start.3 = (f32[8,384]{1,0:T(8,128)S(1)}, f32[8,384]{1,0:T(8,128)}, u32[]{:S(2)}) copy-start(f32[8,384]{1,0:T(8,128)} %across.7) | copy-start | bytes 36868
  73.8 26.7 %collective-permute-start.10 = (f32[2,128,768]{2,1,0:T(8,128)S(1)}, f32[2,128,768]{2,1,0:T(8,128)S(1)}, u32[]{:S(2)}, u32[]{:S(2)}) collective-permute-start(f32[2,128,768]{2,1,0:T(8,128)S(1)} %broadcast_select_fusion.1), channel_id=1, source_target_pairs={{0,1},{1,0},{2,3},{3,2},{4,5},{5,4},{6,7},{7,6},{8,9},{9,8},{10,11... | collective-permute-start | bytes 2359304 | tf_op jit(solution)/shard_map/ppermute | solution.py:475
  97.3 4.4 %collective-permute-start.11 = (f32[2,128,768]{2,1,0:T(8,128)S(1)}, f32[2,128,768]{2,1,0:T(8,128)}, u32[]{:S(2)}, u32[]{:S(2)}) collective-permute-start(f32[2,128,768]{2,1,0:T(8,128)S(1)} %broadcast_select_fusion), channel_id=1, source_target_pairs={{0,1},{1,0},{2,3},{3,2},{4,5},{5,4},{6,7},{7,6},{8,9},{9,8},{10,11... | collective-permute-start | bytes 2359304 | tf_op jit(solution)/shard_map/ppermute | solution.py:475
  100.5 1.2 copy-start.1
  131.7 15.0 %collective-permute-start.14 = (f32[8,384,384]{2,1,0:T(8,128)}, f32[8,384,384]{2,1,0:T(8,128)}, u32[]{:S(2)}, u32[]{:S(2)}) collective-permute-start(f32[8,384,384]{2,1,0:T(8,128)} %get-tuple-element.48.t.own), channel_id=1, source_target_pairs={{0,1},{1,0},{2,3},{3,2},{4,5},{5,4},{6,7},{7,6},{8,9},{9,8},{10,11... | collective-permute-start | bytes 14155784 | tf_op jit(solution)/shard_map/ppermute | solution.py:475
  131.8 47.8 %collective-permute-start.16 = (f32[3,384,384]{2,1,0:T(8,128)}, f32[3,384,384]{2,1,0:T(8,128)}, u32[]{:S(2)}, u32[]{:S(2)}) collective-permute-start(f32[3,384,384]{2,1,0:T(8,128)} %get-tuple-element.50), channel_id=1, source_target_pairs={{0,31},{1,2},{2,1},{3,4},{4,3},{5,6},{6,5},{7,8},{8,7},{9,10},{10,... | collective-permute-start | bytes 5308424 | tf_op jit(solution)/shard_map/ppermute | solution.py:475
  131.9 60.5 %collective-permute-start.15 = (f32[1,384,384]{2,1,0:T(8,128)}, f32[1,384,384]{2,1,0:T(8,128)S(1)}, u32[]{:S(2)}, u32[]{:S(2)}) collective-permute-start(f32[1,384,384]{2,1,0:T(8,128)} %get-tuple-element.49), channel_id=1, source_target_pairs={{0,31},{1,2},{2,1},{3,4},{4,3},{5,6},{6,5},{7,8},{8,7},{9,10},{10,... | collective-permute-start | bytes 1769480 | tf_op jit(solution)/shard_map/ppermute | solution.py:475
  192.4 0.8 copy-start.2

commit v3 on v2

--- a/solution.py
+++ b/solution.py
@@ -16,7 +16,7 @@
 ANY = pl.BlockSpec(memory_space=pl.ANY)
 SMEM = pl.BlockSpec(memory_space=pltpu.SMEM)
 VMEM = pl.BlockSpec(memory_space=pltpu.VMEM)
-PARAMS = pltpu.CompilerParams(vmem_limit_bytes=63 * 1024 * 1024)
+PARAMS = pltpu.CompilerParams(vmem_limit_bytes=127 * 512 * 1024)
 
 CROSS, ORDER, START, SEND, EARLY, EARLY_COUNT, LEFT, RIGHT, COLUMN, SECTIONS = range(10)
 
@@ -270,14 +270,15 @@
 
     t_copies = [pltpu.make_async_copy(t.at[k], t_buf.at[k], t_sem.at[k]) for k in range(high - low)]
 
+    for copy in t_copies:
+        copy.start()
+
     @pl.when(count > 0)
     def _():
         for copy in fetch(0, 0):
             copy.start()
 
     for copy in t_copies:
-        copy.start()
-    for copy in t_copies:
         copy.wait()
 
     def one(s, carry):
@@ -288,11 +289,14 @@
             for copy in fetch(s + 1, 1 - slot):
                 copy.start()
 
-        for copy in fetch(s, slot):
-            copy.wait()
+        x_copy, *other_copies = fetch(s, slot)
+        x_copy.wait()
         p = pair(s)
         picked = t_buf[plan[CROSS * pairs + p] - low]
-        coupled = before_buf[slot] + project(x_buf[slot], picked, gain[p, column])
+        coupled = project(x_buf[slot], picked, gain[p, column])
+        for copy in other_copies:
+            copy.wait()
+        coupled = before_buf[slot] + coupled
         lane = lax.broadcasted_iota(jnp.int32, down.shape, 1)
         tall = jnp.sum(jnp.where(lane == p, down[...], 0.0), axis=1, keepdims=True)
         denominator = tall + across[pl.ds(p, 1), :] - occ[p]

time: 201 us -> 199 us (0.990)
  the two profiles are of different devices: /device:TPU:5 before, /device:TPU:1 now
where the time goes in v3:
time: 199 us; the launch traced here: 197 us
  Pallas kernels  112 us (56%)
  waiting for transfers between devices  48.6 us (24%)
  starting transfers between devices  23.9 us (12%)
  local copies, waits for them, and re-layouts  6 us (3%)
  other arithmetic  5.27 us (3%)
    pallas_call x4, Pallas kernels, couple(): pl.pallas_call(functools.partial(couple_kernel, kind, low, pairs, adding)...  54.4 us
    ppermute x17, waiting for transfers between devices, shards(): send = lambda value, perm: lax.ppermute(value, axis, perm)  48.6 us
    pallas_call x4, Pallas kernels, finish(): pl.pallas_call(functools.partial(finish_kernel, low, high, sending), out_...  36.9 us
    ppermute x17, starting transfers between devices, shards(): send = lambda value, perm: lax.ppermute(value, axis, perm)  23.9 us
    pallas_call x2, Pallas kernels, pair_integrals(): pl.pallas_call(functools.partial(integrals_kernel, early, [len(group) for...  16.3 us
    select_n x3, other arithmetic, shards(): jnp.where(selects_near, n, f)  4.6 us
  transfers between devices with their start and end apart: 17, of which 6 were waited for; matrix products, arithmetic and copies ran while one was open for 6% of the time, Pallas kernels for 49%

profile of v3, /device:TPU:1, one launch (start us, length us, event | category | flops | bytes accessed | tf_op | source)
XLA Modules:
  0.0 196.5 jit_solution(556834865084488370)
XLA Ops:
  0.0 0.1 collective-permute-start.5
  0.1 0.8 copy.16.couplings
  0.8 2.6 %collective-permute-start = (s32[8,3]{1,0:T(8,128)S(1)}, s32[8,3]{1,0:T(8,128)S(1)}, u32[]{:S(2)}, u32[]{:S(2)}) collective-permute-start(s32[8,3]{1,0:T(8,128)S(1)} %copy.16.couplings), channel_id=1, source_target_pairs={{0,31},{1,2},{2,1},{3,4},{4,3},{5,6},{6,5},{7,8},{8,7},{9,10},{10,... | collective-permute-start | bytes 296 | tf_op jit(solution)/shard_map/ppermute | solution.py:479
  3.4 4.4 %collective-permute-start.8 = (f32[2,384,768]{2,1,0:T(8,128)}, f32[2,384,768]{2,1,0:T(8,128)}, u32[]{:S(2)}, u32[]{:S(2)}) collective-permute-start(f32[2,384,768]{2,1,0:T(8,128)} %slabs.3), channel_id=1, source_target_pairs={{0,1},{1,0},{2,3},{3,2},{4,5},{5,4},{6,7},{7,6},{8,9},{9,8},{10,11... | collective-permute-start | bytes 7077896 | tf_op jit(solution)/shard_map/ppermute | solution.py:479
  7.9 3.1 %fusion.2 = (f32[2,128,768]{2,1,0:T(8,128)}, f32[2,128,768]{2,1,0:T(8,128)}, f32[2,128,768]{2,1,0:T(8,128)}) fusion(f32[2,384,768]{2,1,0:T(8,128)} %slabs.3), kind=kLoop, calls=%fused_computation.8 | loop fusion | bytes 4718592 | tf_op jit(solution)/shard_map/slice | solution.py:483
  10.9 0.0 collective-permute-done.lists_cross
  11.0 0.7 copy.17.gain
  11.6 1.4 collective-permute-start.4
  13.1 0.7 pad_add_fusion.rows
  13.7 0.0 collective-permute-start.1
  13.8 13.2 %couple.4.rest_0_ = f32[8,384,384]{2,1,0:T(8,128)} custom-call(s32[18]{0:T(128)} %pad_add_fusion.rows, f32[8,3,384,384]{3,2,1,0:T(8,128)} %x.15, f32[8,384,384]{2,1,0:T(8,128)} %own.3, f32[8,3]{1,0:T(8,128)} %copy.17.gain), custom_call_target="tpu_custom_call" | custom-call | flops 5435817 | bytes 14155 | tf_op jit(solution)/shard_map/couple/pallas_call | solution.py:231
  27.0 0.0 copy-start.5
  27.0 3.4 %collective-permute-done.2.rest_1_ = f32[2,128,768]{2,1,0:T(8,128)} collective-permute-done((f32[2,128,768]{2,1,0:T(8,128)}, f32[2,128,768]{2,1,0:T(8,128)}, u32[]{:S(2)}, u32[]{:S(2)}) %collective-permute-start.2) | collective-permute-done | bytes 786464 | tf_op jit(solution)/shard_map/ppermute | solution.py:479
  30.4 0.0 collective-permute-start.3
  30.4 14.0 %couple.5.before = f32[8,384,384]{2,1,0:T(8,128)} custom-call(s32[18]{0:T(128)} %pad_add_fusion.rows, f32[8,3,384,384]{3,2,1,0:T(8,128)} %x.15, f32[8,384,384]{2,1,0:T(8,128)} %collective-permute-done.5.t, f32[8,3]{1,0:T(8,128)} %copy.17.gain, f32[8,384,384]{2,1,0:T(8,128)} %couple.4.rest_0_), custom_call_target="tpu_custom_call", output_to_operand_aliasing={{}: (4, {})} | custom-call | flops 5435817 | bytes 14155 | tf_op jit(solution)/shard_map/couple/pallas_call | solution.py:231
  44.4 2.8 %collective-permute-done.4.rest_2_ = f32[2,128,768]{2,1,0:T(8,128)} collective-permute-done((f32[2,128,768]{2,1,0:T(8,128)}, f32[2,128,768]{2,1,0:T(8,128)}, u32[]{:S(2)}, u32[]{:S(2)}) %collective-permute-start.4) | collective-permute-done | bytes 786464 | tf_op jit(solution)/shard_map/ppermute | solution.py:479
  47.3 0.7 copy.20.pair_orbs
  47.9 1.6 plan.1
  49.6 3.3 %gather_rows.1 = (f32[2,384,384]{2,1,0:T(8,128)}, f32[2,384,384]{2,1,0:T(8,128)}) custom-call(s32[72]{0:T(128)} %plan.1, f32[8,384,384]{2,1,0:T(8,128)} %own.3), custom_call_target="tpu_custom_call" | custom-call | bytes 4718 | tf_op jit(solution)/shard_map/gather_rows/pallas_call | solution.py:197
  52.9 11.2 %collective-permute-done.1.rest_3_ = f32[2,128,768]{2,1,0:T(8,128)} collective-permute-done((f32[2,128,768]{2,1,0:T(8,128)}, f32[2,128,768]{2,1,0:T(8,128)}, u32[]{:S(2)}, u32[]{:S(2)}) %collective-permute-start.1) | collective-permute-done | bytes 786464 | tf_op jit(solution)/shard_map/ppermute | solution.py:479
  64.1 0.7 collective-permute-start.13
  64.8 1.1 collective-permute-start.12
  65.9 2.1 %broadcast_select_fusion.2 = f32[2,128,768]{2,1,0:T(8,128)} fusion(f32[2,128,768]{2,1,0:T(8,128)} %collective-permute-done.2.rest_1_, f32[2,128,768]{2,1,0:T(8,128)} %collective-permute-done.3.rest_0_, pred[]{:T(512)S(6)} %eq.11), kind=kLoop, calls=%fused_computation.2 | loop fusion | flops 196608 | bytes 2359297 | tf_op jit(solution)/shard_map/jit(_where)/select_n | solution.py:512
  68.0 0.0 collective-permute-done.8.rest_0_
  68.0 4.4 %collective-permute-start.9 = (f32[2,128,768]{2,1,0:T(8,128)}, f32[2,128,768]{2,1,0:T(8,128)}, u32[]{:S(2)}, u32[]{:S(2)}) collective-permute-start(f32[2,128,768]{2,1,0:T(8,128)} %broadcast_select_fusion.2), channel_id=1, source_target_pairs={{0,1},{1,0},{2,3},{3,2},{4,5},{5,4},{6,7},{7,6},{8,9},{9,8},{10,11... | collective-permute-start | bytes 2359304 | tf_op jit(solution)/shard_map/ppermute | solution.py:479
  72.4 9.4 %pair_integrals.2.rest_6_ = f32[8,384,384]{2,1,0:T(8,128)} custom-call(s32[72]{0:T(128)} %plan.1, f32[2,384,768]{2,1,0:T(8,128)} %slabs.3, f32[2,384,768]{2,1,0:T(8,128)} %collective-permute-done.8.rest_0_, f32[2,128,768]{2,1,0:T(8,128)} %collective-permute-done.2.rest_1_, f32[2,128,768]{2,1,0:T(8,128)} %collective-permute-done.4.rest_2_, ...), custom_call_target="tpu_custom_call" | custom-call | flops 2717908 | bytes 4718 | tf_op jit(solution)/shard_map/pair_integrals/pallas_call | solution.py:442
  81.8 0.0 copy-start
  81.8 0.0 collective-permute-done.6.rest_1_
  81.8 1.2 broadcast_select_fusion.1
  83.1 3.8 %collective-permute-start.10 = (f32[2,128,768]{2,1,0:T(8,128)S(1)}, f32[2,128,768]{2,1,0:T(8,128)}, u32[]{:S(2)}, u32[]{:S(2)}) collective-permute-start(f32[2,128,768]{2,1,0:T(8,128)S(1)} %broadcast_select_fusion.1), channel_id=1, source_target_pairs={{0,1},{1,0},{2,3},{3,2},{4,5},{5,4},{6,7},{7,6},{8,9},{9,8},{10,11... | collective-permute-start | bytes 2359304 | tf_op jit(solution)/shard_map/ppermute | solution.py:479
  86.9 13.7 %collective-permute-done.7.rest_2_ = f32[2,128,768]{2,1,0:T(8,128)} collective-permute-done((f32[2,128,768]{2,1,0:T(8,128)}, f32[2,128,768]{2,1,0:T(8,128)}, u32[]{:S(2)}, u32[]{:S(2)}) %collective-permute-start.7) | collective-permute-done | bytes 786464 | tf_op jit(solution)/shard_map/ppermute | solution.py:479
  100.6 1.2 broadcast_select_fusion
  101.8 3.5 %collective-permute-start.11 = (f32[2,128,768]{2,1,0:T(8,128)S(1)}, f32[2,128,768]{2,1,0:T(8,128)}, u32[]{:S(2)}, u32[]{:S(2)}) collective-permute-start(f32[2,128,768]{2,1,0:T(8,128)S(1)} %broadcast_select_fusion), channel_id=1, source_target_pairs={{0,1},{1,0},{2,3},{3,2},{4,5},{5,4},{6,7},{7,6},{8,9},{9,8},{10,11... | collective-permute-start | bytes 2359304 | tf_op jit(solution)/shard_map/ppermute | solution.py:479
  105.3 0.8 copy.21
  106.1 0.0 collective-permute-done.9.rest_3_
  106.1 0.0 collective-permute-done.10.rest_4_
  106.1 1.2 collective-permute-done.11.rest_5_
  107.3 6.9 %pair_integrals.3.integral = f32[8,384,384]{2,1,0:T(8,128)} custom-call(s32[72]{0:T(128)} %plan.1, f32[2,384,768]{2,1,0:T(8,128)} %slabs.3, f32[2,128,768]{2,1,0:T(8,128)} %collective-permute-done.3.rest_0_, f32[2,128,768]{2,1,0:T(8,128)} %collective-permute-done.6.rest_1_, ...), custom_call_target="tpu_custom_call", output_to_operand_aliasing={{}: (8, {})} | custom-call | flops 2717908 | bytes 4718 | tf_op jit(solution)/shard_map/pair_integrals/pallas_call | solution.py:442
  114.3 9.1 %finish.4 = (f32[8,384,384]{2,1,0:T(8,128)}, f32[3,384,384]{2,1,0:T(8,128)}, f32[1,384,384]{2,1,0:T(8,128)}) custom-call(s32[72]{0:T(128)} %plan.1, f32[8,3]{1,0:T(8,128)} %copy.17.gain, f32[8]{0:T(128)} %occ.7, f32[8,384]{1,0:T(8,128)} %across.7, f32[384,8]{1,0:T(8,128)} %bitcast.7, f32[8,3,384,384]{3,2,1,0:T(8,128)} %x.15, f32[8,384,384]{2,1,0:T(8,128)} %couple.5.before, ...), custom_call_target="tpu_custom_call" | custom-call | flops 2717908 | bytes 14155 | tf_op jit(solution)/shard_map/finish/pallas_call | solution.py:332
  123.4 9.6 %finish.5 = (f32[8,384,384]{2,1,0:T(8,128)}, f32[3,384,384]{2,1,0:T(8,128)}, f32[1,384,384]{2,1,0:T(8,128)}) custom-call(s32[72]{0:T(128)} %plan.1, f32[8,3]{1,0:T(8,128)} %copy.17.gain, f32[8]{0:T(128)} %occ.7, f32[8,384]{1,0:T(8,128)} %across.7, f32[384,8]{1,0:T(8,128)} %bitcast.8, ...), custom_call_target="tpu_custom_call", output_to_operand_aliasing={{0}: (10, {}), {1}: (11, {}), {2}: (12, {})} | custom-call | flops 2717908 | bytes 14155 | tf_op jit(solution)/shard_map/finish/pallas_call | solution.py:332
  132.9 0.1 collective-permute-start.14
  133.0 0.1 collective-permute-start.16
  133.1 1.7 collective-permute-start.15
  134.8 13.2 %couple.6.rest_0_ = f32[8,384,384]{2,1,0:T(8,128)} custom-call(s32[18]{0:T(128)} %pad_add_fusion.rows, f32[8,3,384,384]{3,2,1,0:T(8,128)} %x.15, f32[8,384,384]{2,1,0:T(8,128)} %get-tuple-element.48.t.own, f32[8,3]{1,0:T(8,128)} %copy.17.gain), custom_call_target="tpu_custom_call" | custom-call | flops 5435817 | bytes 14155 | tf_op jit(solution)/shard_map/couple/pallas_call | solution.py:231
  148.0 14.0 %couple.7.before = f32[8,384,384]{2,1,0:T(8,128)} custom-call(s32[18]{0:T(128)} %pad_add_fusion.rows, f32[8,3,384,384]{3,2,1,0:T(8,128)} %x.15, f32[8,384,384]{2,1,0:T(8,128)} %collective-permute-done.14.t, f32[8,3]{1,0:T(8,128)} %copy.17.gain, f32[8,384,384]{2,1,0:T(8,128)} %couple.6.rest_0_), custom_call_target="tpu_custom_call", output_to_operand_aliasing={{}: (4, {})} | custom-call | flops 5435817 | bytes 14155 | tf_op jit(solution)/shard_map/couple/pallas_call | solution.py:231
  162.0 16.1 %collective-permute-done.16.rest_0_ = f32[3,384,384]{2,1,0:T(8,128)} collective-permute-done((f32[3,384,384]{2,1,0:T(8,128)}, f32[3,384,384]{2,1,0:T(8,128)}, u32[]{:S(2)}, u32[]{:S(2)}) %collective-permute-start.16) | collective-permute-done | bytes 1769504 | tf_op jit(solution)/shard_map/ppermute | solution.py:479
  178.2 12.1 %finish.6.rest_1_ = f32[8,384,384]{2,1,0:T(8,128)} custom-call(s32[72]{0:T(128)} %plan.1, f32[8,3]{1,0:T(8,128)} %copy.17.gain, f32[8]{0:T(128)} %occ.7, f32[8,384]{1,0:T(8,128)} %across.7, f32[384,8]{1,0:T(8,128)} %bitcast.9, f32[8,3,384,384]{3,2,1,0:T(8,128)} %x.15, f32[8,384,384]{2,1,0:T(8,128)} %couple.7.before, f32[8,384,384]{2,1,0:T(8,128)} %pair_integrals.3.integral, ...), custom_call_target="tpu_custom_call" | custom-call | flops 4076863 | bytes 21233 | tf_op jit(solution)/shard_map/finish/pallas_call | solution.py:332
  190.3 6.1 %finish.7 = f32[8,384,384]{2,1,0:T(8,128)} custom-call(s32[72]{0:T(128)} %plan.1, f32[8,3]{1,0:T(8,128)} %copy.17.gain, f32[8]{0:T(128)} %occ.7, f32[8,384]{1,0:T(8,128)} %across.7, f32[384,8]{1,0:T(8,128)} %bitcast.10, f32[8,3,384,384]{3,2,1,0:T(8,128)} %x.15, f32[8,384,384]{2,1,0:T(8,128)} %couple.7.before, ...), custom_call_target="tpu_custom_call", output_to_operand_aliasing={{}: (10, {})} | custom-call | flops 1358954 | bytes 7077 | tf_op jit(solution)/shard_map/finish/pallas_call | solution.py:332
  (20 shorter events, 0.0 us)
Async XLA Ops:
  0.0 13.1 %copy-start.2 = (s32[8,3]{0,1:T(4,128)S(1)}, s32[8,3]{0,1:T(4,128)}, u32[]{:S(2)}) copy-start(s32[8,3]{0,1:T(4,128)} %param.15) | copy-start | bytes 292
  0.0 11.0 %copy-start.4 = (f32[8,3]{0,1:T(4,128)S(1)}, f32[8,3]{0,1:T(4,128)}, u32[]{:S(2)}) copy-start(f32[8,3]{0,1:T(4,128)} %param.11) | copy-start | bytes 292
  0.0 30.4 %collective-permute-start.5 = (f32[8,384,384]{2,1,0:T(8,128)}, f32[8,384,384]{2,1,0:T(8,128)}, u32[]{:S(2)}, u32[]{:S(2)}) collective-permute-start(f32[8,384,384]{2,1,0:T(8,128)} %own.3), channel_id=1, source_target_pairs={{0,1},{1,0},{2,3},{3,2},{4,5},{5,4},{6,7},{7,6},{8,9},{9,8},{10,11... | collective-permute-start | bytes 14155784 | tf_op jit(solution)/shard_map/ppermute | solution.py:479
  0.8 26.1 %copy-start.1 = (s32[8,3]{1,0:T(8,128)}, s32[8,3]{1,0:T(8,128)S(1)}, u32[]{:S(2)}) copy-start(s32[8,3]{1,0:T(8,128)S(1)} %copy.16.couplings) | copy-start | bytes 292
  0.8 10.1 %collective-permute-start = (s32[8,3]{1,0:T(8,128)S(1)}, s32[8,3]{1,0:T(8,128)S(1)}, u32[]{:S(2)}, u32[]{:S(2)}) collective-permute-start(s32[8,3]{1,0:T(8,128)S(1)} %copy.16.couplings), channel_id=1, source_target_pairs={{0,31},{1,2},{2,1},{3,4},{4,3},{5,6},{6,5},{7,8},{8,7},{9,10},{10,... | collective-permute-start | bytes 296 | tf_op jit(solution)/shard_map/ppermute | solution.py:479
  3.4 64.6 %collective-permute-start.8 = (f32[2,384,768]{2,1,0:T(8,128)}, f32[2,384,768]{2,1,0:T(8,128)}, u32[]{:S(2)}, u32[]{:S(2)}) collective-permute-start(f32[2,384,768]{2,1,0:T(8,128)} %slabs.3), channel_id=1, source_target_pairs={{0,1},{1,0},{2,3},{3,2},{4,5},{5,4},{6,7},{7,6},{8,9},{9,8},{10,11... | collective-permute-start | bytes 7077896 | tf_op jit(solution)/shard_map/ppermute | solution.py:479
  10.9 16.0 %copy-start.3 = (s32[8,3]{1,0:T(8,128)}, s32[8,3]{1,0:T(8,128)S(1)}, u32[]{:S(2)}) copy-start(s32[8,3]{1,0:T(8,128)S(1)} %collective-permute-done.lists_cross) | copy-start | bytes 292
  10.9 19.5 %collective-permute-start.2 = (f32[2,128,768]{2,1,0:T(8,128)}, f32[2,128,768]{2,1,0:T(8,128)}, u32[]{:S(2)}, u32[]{:S(2)}) collective-permute-start(f32[2,128,768]{2,1,0:T(8,128)} %get-tuple-element.29), channel_id=1, source_target_pairs={{0,2},{1,3},{2,0},{3,1},{4,6},{5,7},{6,4},{7,5},{8,10},{9,11},{10,... | collective-permute-start | bytes 2359304 | tf_op jit(solution)/shard_map/ppermute | solution.py:479
  11.6 35.6 %collective-permute-start.4 = (f32[2,128,768]{2,1,0:T(8,128)}, f32[2,128,768]{2,1,0:T(8,128)}, u32[]{:S(2)}, u32[]{:S(2)}) collective-permute-start(f32[2,128,768]{2,1,0:T(8,128)} %get-tuple-element.30), channel_id=1, source_target_pairs={{0,2},{1,3},{2,0},{3,1},{4,6},{5,7},{6,4},{7,5},{8,10},{9,11},{10,... | collective-permute-start | bytes 2359304 | tf_op jit(solution)/shard_map/ppermute | solution.py:479
  13.7 50.4 %collective-permute-start.1 = (f32[2,128,768]{2,1,0:T(8,128)}, f32[2,128,768]{2,1,0:T(8,128)}, u32[]{:S(2)}, u32[]{:S(2)}) collective-permute-start(f32[2,128,768]{2,1,0:T(8,128)} %get-tuple-element.28), channel_id=1, source_target_pairs={{0,2},{1,3},{2,0},{3,1},{4,6},{5,7},{6,4},{7,5},{8,10},{9,11},{10,... | collective-permute-start | bytes 2359304 | tf_op jit(solution)/shard_map/ppermute | solution.py:479
  27.0 20.3 %copy-start.5 = (s32[8,2]{0,1:T(2,128)S(1)}, s32[8,2]{0,1:T(2,128)}, u32[]{:S(2)}) copy-start(s32[8,2]{0,1:T(2,128)} %param.14) | copy-start | bytes 196
  30.4 33.7 %collective-permute-start.3 = (f32[2,128,768]{2,1,0:T(8,128)}, f32[2,128,768]{2,1,0:T(8,128)}, u32[]{:S(2)}, u32[]{:S(2)}) collective-permute-start(f32[2,128,768]{2,1,0:T(8,128)} %collective-permute-done.2.rest_1_), channel_id=1, source_target_pairs={{0,4},{1,5},{2,30},{3,31},{4,8},{5,9},{6,2},{7,3},{8,12},{9,13},{1... | collective-permute-start | bytes 2359304 | tf_op jit(solution)/shard_map/ppermute | solution.py:479
  47.3 34.6 %collective-permute-start.6 = (f32[2,128,768]{2,1,0:T(8,128)}, f32[2,128,768]{2,1,0:T(8,128)}, u32[]{:S(2)}, u32[]{:S(2)}) collective-permute-start(f32[2,128,768]{2,1,0:T(8,128)} %collective-permute-done.4.rest_2_), channel_id=1, source_target_pairs={{0,4},{1,5},{2,30},{3,31},{4,8},{5,9},{6,2},{7,3},{8,12},{9,13},{1... | collective-permute-start | bytes 2359304 | tf_op jit(solution)/shard_map/ppermute | solution.py:479
  64.1 36.5 %collective-permute-start.7 = (f32[2,128,768]{2,1,0:T(8,128)}, f32[2,128,768]{2,1,0:T(8,128)}, u32[]{:S(2)}, u32[]{:S(2)}) collective-permute-start(f32[2,128,768]{2,1,0:T(8,128)} %collective-permute-done.1.rest_3_), channel_id=1, source_target_pairs={{0,4},{1,5},{2,30},{3,31},{4,8},{5,9},{6,2},{7,3},{8,12},{9,13},{1... | collective-permute-start | bytes 2359304 | tf_op jit(solution)/shard_map/ppermute | solution.py:479
  64.1 50.1 %collective-permute-start.13 = (f32[2,384,384]{2,1,0:T(8,128)}, f32[2,384,384]{2,1,0:T(8,128)}, u32[]{:S(2)}, u32[]{:S(2)}) collective-permute-start(f32[2,384,384]{2,1,0:T(8,128)} %get-tuple-element.37), channel_id=1, source_target_pairs={{0,31},{1,2},{2,1},{3,4},{4,3},{5,6},{6,5},{7,8},{8,7},{9,10},{10,... | collective-permute-start | bytes 3538952 | tf_op jit(solution)/shard_map/ppermute | solution.py:479
  64.8 58.6 %collective-permute-start.12 = (f32[2,384,384]{2,1,0:T(8,128)}, f32[2,384,384]{2,1,0:T(8,128)}, u32[]{:S(2)}, u32[]{:S(2)}) collective-permute-start(f32[2,384,384]{2,1,0:T(8,128)} %get-tuple-element.38), channel_id=1, source_target_pairs={{0,31},{1,2},{2,1},{3,4},{4,3},{5,6},{6,5},{7,8},{8,7},{9,10},{10,... | collective-permute-start | bytes 3538952 | tf_op jit(solution)/shard_map/ppermute | solution.py:479
  68.0 38.1 %collective-permute-start.9 = (f32[2,128,768]{2,1,0:T(8,128)}, f32[2,128,768]{2,1,0:T(8,128)}, u32[]{:S(2)}, u32[]{:S(2)}) collective-permute-start(f32[2,128,768]{2,1,0:T(8,128)} %broadcast_select_fusion.2), channel_id=1, source_target_pairs={{0,1},{1,0},{2,3},{3,2},{4,5},{5,4},{6,7},{7,6},{8,9},{9,8},{10,11... | collective-permute-start | bytes 2359304 | tf_op jit(solution)/shard_map/ppermute | solution.py:479
  81.8 23.5 %copy-start = (f32[8,384]{1,0:T(8,128)S(1)}, f32[8,384]{1,0:T(8,128)}, u32[]{:S(2)}) copy-start(f32[8,384]{1,0:T(8,128)} %across.7) | copy-start | bytes 36868
  83.1 23.0 %collective-permute-start.10 = (f32[2,128,768]{2,1,0:T(8,128)S(1)}, f32[2,128,768]{2,1,0:T(8,128)}, u32[]{:S(2)}, u32[]{:S(2)}) collective-permute-start(f32[2,128,768]{2,1,0:T(8,128)S(1)} %broadcast_select_fusion.1), channel_id=1, source_target_pairs={{0,1},{1,0},{2,3},{3,2},{4,5},{5,4},{6,7},{7,6},{8,9},{9,8},{10,11... | collective-permute-start | bytes 2359304 | tf_op jit(solution)/shard_map/ppermute | solution.py:479
  101.8 5.5 %collective-permute-start.11 = (f32[2,128,768]{2,1,0:T(8,128)S(1)}, f32[2,128,768]{2,1,0:T(8,128)}, u32[]{:S(2)}, u32[]{:S(2)}) collective-permute-start(f32[2,128,768]{2,1,0:T(8,128)S(1)} %broadcast_select_fusion), channel_id=1, source_target_pairs={{0,1},{1,0},{2,3},{3,2},{4,5},{5,4},{6,7},{7,6},{8,9},{9,8},{10,11... | collective-permute-start | bytes 2359304 | tf_op jit(solution)/shard_map/ppermute | solution.py:479
  132.9 15.1 %collective-permute-start.14 = (f32[8,384,384]{2,1,0:T(8,128)}, f32[8,384,384]{2,1,0:T(8,128)}, u32[]{:S(2)}, u32[]{:S(2)}) collective-permute-start(f32[8,384,384]{2,1,0:T(8,128)} %get-tuple-element.48.t.own), channel_id=1, source_target_pairs={{0,1},{1,0},{2,3},{3,2},{4,5},{5,4},{6,7},{7,6},{8,9},{9,8},{10,11... | collective-permute-start | bytes 14155784 | tf_op jit(solution)/shard_map/ppermute | solution.py:479
  133.0 45.1 %collective-permute-start.16 = (f32[3,384,384]{2,1,0:T(8,128)}, f32[3,384,384]{2,1,0:T(8,128)}, u32[]{:S(2)}, u32[]{:S(2)}) collective-permute-start(f32[3,384,384]{2,1,0:T(8,128)} %get-tuple-element.50), channel_id=1, source_target_pairs={{0,31},{1,2},{2,1},{3,4},{4,3},{5,6},{6,5},{7,8},{8,7},{9,10},{10,... | collective-permute-start | bytes 5308424 | tf_op jit(solution)/shard_map/ppermute | solution.py:479
  133.1 57.2 %collective-permute-start.15 = (f32[1,384,384]{2,1,0:T(8,128)}, f32[1,384,384]{2,1,0:T(8,128)}, u32[]{:S(2)}, u32[]{:S(2)}) collective-permute-start(f32[1,384,384]{2,1,0:T(8,128)} %get-tuple-element.49), channel_id=1, source_target_pairs={{0,31},{1,2},{2,1},{3,4},{4,3},{5,6},{6,5},{7,8},{8,7},{9,10},{10,... | collective-permute-start | bytes 1769480 | tf_op jit(solution)/shard_map/ppermute | solution.py:479

commit v4 on v3

--- a/solution.py
+++ b/solution.py
@@ -504,12 +504,14 @@
     plan = make_plan(count, orbitals, where, couplings, lists_cross, pair_orbs)
     across, down = virt_energy, virt_energy.T
     cross_out = gather_rows(plan, amplitudes)
+    near[2], far[0], plan, *cross_out = lax.optimization_barrier((near[2], far[0], plan, *cross_out))
+    far.append(send(near[2], far_perm))
+    chosen = jnp.where(selects_near, near[0], far[0])
+    chosen, *cross_out = lax.optimization_barrier((chosen, *cross_out))
     cross_t = [send(rows_out, beside) for rows_out in cross_out]
-    near[2], far[0], plan, *_ = lax.optimization_barrier((near[2], far[0], plan, *cross_out))
-    far.append(send(near[2], far_perm))
     integrals = pair_integrals(True, plan, slabs, pairs, [[slabs_swapped], near])
     far[2], integrals = lax.optimization_barrier((far[2], integrals))
-    relayed = [send(jnp.where(selects_near, n, f), inside) for n, f in zip(near, far)]
+    relayed = [send(chosen, inside)] + [send(jnp.where(selects_near, n, f), inside) for n, f in zip(near[1:], far[1:])]
     integrals = pair_integrals(False, plan, slabs, pairs, [far, relayed], integrals)
 
     current = amplitudes
@@ -521,7 +523,8 @@
             partial = couple(1, 0, pairs, coupled_rows, intersections, intra_t, fock_coupling, partial, True)
         sending = iteration + 1 < ITERS
         done = None
-        for k, (low, high) in enumerate(rank_groups(half, iteration)):
+        groups = list(enumerate(rank_groups(half, iteration)))
+        for k, (low, high) in groups if iteration > 0 else groups[::-1]:
             done = finish(
                 low,
                 high,

time: 199 us -> 206 us (1.035)
  waiting for transfers between devices: 48.6 us -> 58 us
    ppermute x17, waiting for transfers between devices: 48.6 us -> 58 us  [shards(): send = lambda value, perm: lax.ppermute(value, axis, perm)]
    select_n x0 -> x1, other arithmetic: none -> 2.14 us  [shards(): chosen = jnp.where(selects_near, near[0], far[0])]
    select_n x3 -> x2, other arithmetic: 4.6 us -> 2.47 us  [shards(): jnp.where(selects_near, n, f)]
  transfers between devices with their start and end apart: 17 -> 17, of which waited for: 6 -> 7; matrix products, arithmetic and copies ran while one was open for 6% -> 6% of each run, Pallas kernels for 49% -> 48%
where the time goes in v4:
time: 206 us; the launch traced here: 204 us
  Pallas kernels  112 us (54%)
  waiting for transfers between devices  58 us (28%)
  starting transfers between devices  22.1 us (11%)
  local copies, waits for them, and re-layouts  6 us (3%)
  other arithmetic  5.28 us (3%)
    ppermute x17, waiting for transfers between devices, shards(): send = lambda value, perm: lax.ppermute(value, axis, perm)  58 us
    pallas_call x4, Pallas kernels, couple(): pl.pallas_call(functools.partial(couple_kernel, kind, low, pairs, adding)...  54.4 us
    pallas_call x4, Pallas kernels, finish(): pl.pallas_call(functools.partial(finish_kernel, low, high, sending), out_...  36.8 us
    ppermute x17, starting transfers between devices, shards(): send = lambda value, perm: lax.ppermute(value, axis, perm)  22.1 us
    pallas_call x2, Pallas kernels, pair_integrals(): pl.pallas_call(functools.partial(integrals_kernel, early, [len(group) for...  16.4 us
  transfers between devices with their start and end apart: 17, of which 7 were waited for; matrix products, arithmetic and copies ran while one was open for 6% of the time, Pallas kernels for 48%

profile of v4, /device:TPU:1, one launch (start us, length us, event | category | flops | bytes accessed | tf_op | source)
XLA Modules:
  0.0 204.2 jit_solution(7983791373489812304)
XLA Ops:
  0.0 0.1 collective-permute-start.5
  0.1 0.8 copy.16.couplings
  0.8 2.6 %collective-permute-start = (s32[8,3]{1,0:T(8,128)S(1)}, s32[8,3]{1,0:T(8,128)S(1)}, u32[]{:S(2)}, u32[]{:S(2)}) collective-permute-start(s32[8,3]{1,0:T(8,128)S(1)} %copy.16.couplings), channel_id=1, source_target_pairs={{0,31},{1,2},{2,1},{3,4},{4,3},{5,6},{6,5},{7,8},{8,7},{9,10},{10,... | collective-permute-start | bytes 296 | tf_op jit(solution)/shard_map/ppermute | solution.py:479
  3.4 4.4 %collective-permute-start.8 = (f32[2,384,768]{2,1,0:T(8,128)}, f32[2,384,768]{2,1,0:T(8,128)}, u32[]{:S(2)}, u32[]{:S(2)}) collective-permute-start(f32[2,384,768]{2,1,0:T(8,128)} %slabs.3), channel_id=1, source_target_pairs={{0,1},{1,0},{2,3},{3,2},{4,5},{5,4},{6,7},{7,6},{8,9},{9,8},{10,11... | collective-permute-start | bytes 7077896 | tf_op jit(solution)/shard_map/ppermute | solution.py:479
  7.9 3.1 %fusion.2 = (f32[2,128,768]{2,1,0:T(8,128)}, f32[2,128,768]{2,1,0:T(8,128)}, f32[2,128,768]{2,1,0:T(8,128)}) fusion(f32[2,384,768]{2,1,0:T(8,128)} %slabs.3), kind=kLoop, calls=%fused_computation.8 | loop fusion | bytes 4718592 | tf_op jit(solution)/shard_map/slice | solution.py:483
  11.0 0.7 copy.17.gain
  11.6 1.4 collective-permute-start.4
  13.1 0.7 pad_add_fusion.rows
  13.7 0.0 collective-permute-start.1
  13.8 13.2 %couple.4.rest_0_ = f32[8,384,384]{2,1,0:T(8,128)} custom-call(s32[18]{0:T(128)} %pad_add_fusion.rows, f32[8,3,384,384]{3,2,1,0:T(8,128)} %x.15, f32[8,384,384]{2,1,0:T(8,128)} %own.3, f32[8,3]{1,0:T(8,128)} %copy.17.gain), custom_call_target="tpu_custom_call" | custom-call | flops 5435817 | bytes 14155 | tf_op jit(solution)/shard_map/couple/pallas_call | solution.py:231
  27.0 0.0 copy-start.5
  27.0 3.4 %collective-permute-done.2.rest_1_ = f32[2,128,768]{2,1,0:T(8,128)} collective-permute-done((f32[2,128,768]{2,1,0:T(8,128)}, f32[2,128,768]{2,1,0:T(8,128)}, u32[]{:S(2)}, u32[]{:S(2)}) %collective-permute-start.2) | collective-permute-done | bytes 786464 | tf_op jit(solution)/shard_map/ppermute | solution.py:479
  30.4 0.0 collective-permute-start.3
  30.4 0.0 collective-permute-done.5.t
  30.4 14.0 %couple.5.before = f32[8,384,384]{2,1,0:T(8,128)} custom-call(s32[18]{0:T(128)} %pad_add_fusion.rows, f32[8,3,384,384]{3,2,1,0:T(8,128)} %x.15, f32[8,384,384]{2,1,0:T(8,128)} %collective-permute-done.5.t, f32[8,3]{1,0:T(8,128)} %copy.17.gain, f32[8,384,384]{2,1,0:T(8,128)} %couple.4.rest_0_), custom_call_target="tpu_custom_call", output_to_operand_aliasing={{}: (4, {})} | custom-call | flops 5435817 | bytes 14155 | tf_op jit(solution)/shard_map/couple/pallas_call | solution.py:231
  44.4 2.8 %collective-permute-done.4.rest_2_ = f32[2,128,768]{2,1,0:T(8,128)} collective-permute-done((f32[2,128,768]{2,1,0:T(8,128)}, f32[2,128,768]{2,1,0:T(8,128)}, u32[]{:S(2)}, u32[]{:S(2)}) %collective-permute-start.4) | collective-permute-done | bytes 786464 | tf_op jit(solution)/shard_map/ppermute | solution.py:479
  47.3 0.0 collective-permute-start.6
  47.3 0.7 copy.20.pair_orbs
  47.9 1.6 plan.1
  49.6 3.3 %gather_rows.1 = (f32[2,384,384]{2,1,0:T(8,128)}, f32[2,384,384]{2,1,0:T(8,128)}) custom-call(s32[72]{0:T(128)} %plan.1, f32[8,384,384]{2,1,0:T(8,128)} %own.3), custom_call_target="tpu_custom_call" | custom-call | bytes 4718 | tf_op jit(solution)/shard_map/gather_rows/pallas_call | solution.py:197
  52.9 11.2 %collective-permute-done.1.rest_3_ = f32[2,128,768]{2,1,0:T(8,128)} collective-permute-done((f32[2,128,768]{2,1,0:T(8,128)}, f32[2,128,768]{2,1,0:T(8,128)}, u32[]{:S(2)}, u32[]{:S(2)}) %collective-permute-start.1) | collective-permute-done | bytes 786464 | tf_op jit(solution)/shard_map/ppermute | solution.py:479
  64.1 2.1 %broadcast_select_fusion.2 = f32[2,128,768]{2,1,0:T(8,128)} fusion(f32[2,128,768]{2,1,0:T(8,128)} %collective-permute-done.2.rest_1_, f32[2,128,768]{2,1,0:T(8,128)} %collective-permute-done.3.rest_0_, pred[]{:T(512)S(6)} %eq.11), kind=kLoop, calls=%fused_computation.2 | loop fusion | flops 196608 | bytes 2359297 | tf_op jit(solution)/shard_map/jit(_where)/select_n | solution.py:509
  66.3 0.8 collective-permute-start.9
  67.0 1.0 collective-permute-start.12
  68.0 0.0 collective-permute-done.8.rest_0_
  68.0 0.7 collective-permute-start.13
  68.8 11.9 %pair_integrals.2.rest_6_ = f32[8,384,384]{2,1,0:T(8,128)} custom-call(s32[72]{0:T(128)} %plan.1, f32[2,384,768]{2,1,0:T(8,128)} %slabs.3, f32[2,384,768]{2,1,0:T(8,128)} %collective-permute-done.8.rest_0_, f32[2,128,768]{2,1,0:T(8,128)} %collective-permute-done.2.rest_1_, f32[2,128,768]{2,1,0:T(8,128)} %collective-permute-done.4.rest_2_, ...), custom_call_target="tpu_custom_call" | custom-call | flops 2717908 | bytes 4718 | tf_op jit(solution)/shard_map/pair_integrals/pallas_call | solution.py:442
  80.7 0.0 copy-start
  80.7 1.2 broadcast_select_fusion.1
  82.0 4.9 %collective-permute-start.10 = (f32[2,128,768]{2,1,0:T(8,128)S(1)}, f32[2,128,768]{2,1,0:T(8,128)}, u32[]{:S(2)}, u32[]{:S(2)}) collective-permute-start(f32[2,128,768]{2,1,0:T(8,128)S(1)} %broadcast_select_fusion.1), channel_id=1, source_target_pairs={{0,1},{1,0},{2,3},{3,2},{4,5},{5,4},{6,7},{7,6},{8,9},{9,8},{10,11... | collective-permute-start | bytes 2359304 | tf_op jit(solution)/shard_map/ppermute | solution.py:479
  86.9 11.3 %collective-permute-done.7.rest_2_ = f32[2,128,768]{2,1,0:T(8,128)} collective-permute-done((f32[2,128,768]{2,1,0:T(8,128)}, f32[2,128,768]{2,1,0:T(8,128)}, u32[]{:S(2)}, u32[]{:S(2)}) %collective-permute-start.7) | collective-permute-done | bytes 786464 | tf_op jit(solution)/shard_map/ppermute | solution.py:479
  98.2 1.2 broadcast_select_fusion
  99.4 3.5 %collective-permute-start.11 = (f32[2,128,768]{2,1,0:T(8,128)S(1)}, f32[2,128,768]{2,1,0:T(8,128)}, u32[]{:S(2)}, u32[]{:S(2)}) collective-permute-start(f32[2,128,768]{2,1,0:T(8,128)S(1)} %broadcast_select_fusion), channel_id=1, source_target_pairs={{0,1},{1,0},{2,3},{3,2},{4,5},{5,4},{6,7},{7,6},{8,9},{9,8},{10,11... | collective-permute-start | bytes 2359304 | tf_op jit(solution)/shard_map/ppermute | solution.py:479
  102.9 0.8 copy.21
  103.7 1.2 collective-permute-done.11.rest_5_
  104.9 4.5 %pair_integrals.3.integral = f32[8,384,384]{2,1,0:T(8,128)} custom-call(s32[72]{0:T(128)} %plan.1, f32[2,384,768]{2,1,0:T(8,128)} %slabs.3, f32[2,128,768]{2,1,0:T(8,128)} %collective-permute-done.3.rest_0_, f32[2,128,768]{2,1,0:T(8,128)} %collective-permute-done.6.rest_1_, ...), custom_call_target="tpu_custom_call", output_to_operand_aliasing={{}: (8, {})} | custom-call | flops 2717908 | bytes 4718 | tf_op jit(solution)/shard_map/pair_integrals/pallas_call | solution.py:442
  109.4 10.2 %collective-permute-done.13.rest_0_ = f32[2,384,384]{2,1,0:T(8,128)} collective-permute-done((f32[2,384,384]{2,1,0:T(8,128)}, f32[2,384,384]{2,1,0:T(8,128)}, u32[]{:S(2)}, u32[]{:S(2)}) %collective-permute-start.13) | collective-permute-done | bytes 1179680 | tf_op jit(solution)/shard_map/ppermute | solution.py:479
  119.6 9.4 %finish.4 = (f32[8,384,384]{2,1,0:T(8,128)}, f32[3,384,384]{2,1,0:T(8,128)}, f32[1,384,384]{2,1,0:T(8,128)}) custom-call(s32[72]{0:T(128)} %plan.1, f32[8,3]{1,0:T(8,128)} %copy.17.gain, f32[8]{0:T(128)} %occ.7, f32[8,384]{1,0:T(8,128)} %across.7, f32[384,8]{1,0:T(8,128)} %bitcast.7, f32[8,3,384,384]{3,2,1,0:T(8,128)} %x.15, f32[8,384,384]{2,1,0:T(8,128)} %couple.5.before, ...), custom_call_target="tpu_custom_call" | custom-call | flops 2717908 | bytes 14155 | tf_op jit(solution)/shard_map/finish/pallas_call | solution.py:332
  129.0 0.0 collective-permute-done.12.rest_0_
  129.0 9.2 %finish.5 = (f32[8,384,384]{2,1,0:T(8,128)}, f32[3,384,384]{2,1,0:T(8,128)}, f32[1,384,384]{2,1,0:T(8,128)}) custom-call(s32[72]{0:T(128)} %plan.1, f32[8,3]{1,0:T(8,128)} %copy.17.gain, f32[8]{0:T(128)} %occ.7, f32[8,384]{1,0:T(8,128)} %across.7, f32[384,8]{1,0:T(8,128)} %bitcast.8, ...), custom_call_target="tpu_custom_call", output_to_operand_aliasing={{0}: (10, {}), {1}: (11, {}), {2}: (12, {})} | custom-call | flops 2717908 | bytes 14155 | tf_op jit(solution)/shard_map/finish/pallas_call | solution.py:332
  138.2 0.1 collective-permute-start.14
  138.3 2.5 %collective-permute-start.16 = (f32[3,384,384]{2,1,0:T(8,128)}, f32[3,384,384]{2,1,0:T(8,128)}, u32[]{:S(2)}, u32[]{:S(2)}) collective-permute-start(f32[3,384,384]{2,1,0:T(8,128)} %get-tuple-element.60), channel_id=1, source_target_pairs={{0,31},{1,2},{2,1},{3,4},{4,3},{5,6},{6,5},{7,8},{8,7},{9,10},{10,... | collective-permute-start | bytes 5308424 | tf_op jit(solution)/shard_map/ppermute | solution.py:479
  140.8 0.1 collective-permute-start.15
  140.9 13.2 %couple.6.rest_0_ = f32[8,384,384]{2,1,0:T(8,128)} custom-call(s32[18]{0:T(128)} %pad_add_fusion.rows, f32[8,3,384,384]{3,2,1,0:T(8,128)} %x.15, f32[8,384,384]{2,1,0:T(8,128)} %get-tuple-element.58.t.own, f32[8,3]{1,0:T(8,128)} %copy.17.gain), custom_call_target="tpu_custom_call" | custom-call | flops 5435817 | bytes 14155 | tf_op jit(solution)/shard_map/couple/pallas_call | solution.py:231
  154.0 14.0 %couple.7.before = f32[8,384,384]{2,1,0:T(8,128)} custom-call(s32[18]{0:T(128)} %pad_add_fusion.rows, f32[8,3,384,384]{3,2,1,0:T(8,128)} %x.15, f32[8,384,384]{2,1,0:T(8,128)} %collective-permute-done.14.t, f32[8,3]{1,0:T(8,128)} %copy.17.gain, f32[8,384,384]{2,1,0:T(8,128)} %couple.6.rest_0_), custom_call_target="tpu_custom_call", output_to_operand_aliasing={{}: (4, {})} | custom-call | flops 5435817 | bytes 14155 | tf_op jit(solution)/shard_map/couple/pallas_call | solution.py:231
  168.0 17.8 %collective-permute-done.16.rest_0_ = f32[3,384,384]{2,1,0:T(8,128)} collective-permute-done((f32[3,384,384]{2,1,0:T(8,128)}, f32[3,384,384]{2,1,0:T(8,128)}, u32[]{:S(2)}, u32[]{:S(2)}) %collective-permute-start.16) | collective-permute-done | bytes 1769504 | tf_op jit(solution)/shard_map/ppermute | solution.py:479
  185.9 12.1 %finish.6.rest_1_ = f32[8,384,384]{2,1,0:T(8,128)} custom-call(s32[72]{0:T(128)} %plan.1, f32[8,3]{1,0:T(8,128)} %copy.17.gain, f32[8]{0:T(128)} %occ.7, f32[8,384]{1,0:T(8,128)} %across.7, f32[384,8]{1,0:T(8,128)} %bitcast.9, f32[8,3,384,384]{3,2,1,0:T(8,128)} %x.15, f32[8,384,384]{2,1,0:T(8,128)} %couple.7.before, f32[8,384,384]{2,1,0:T(8,128)} %pair_integrals.3.integral, ...), custom_call_target="tpu_custom_call" | custom-call | flops 4076863 | bytes 21233 | tf_op jit(solution)/shard_map/finish/pallas_call | solution.py:332
  198.0 6.1 %finish.7 = f32[8,384,384]{2,1,0:T(8,128)} custom-call(s32[72]{0:T(128)} %plan.1, f32[8,3]{1,0:T(8,128)} %copy.17.gain, f32[8]{0:T(128)} %occ.7, f32[8,384]{1,0:T(8,128)} %across.7, f32[384,8]{1,0:T(8,128)} %bitcast.10, f32[8,3,384,384]{3,2,1,0:T(8,128)} %x.15, f32[8,384,384]{2,1,0:T(8,128)} %couple.7.before, ...), custom_call_target="tpu_custom_call", output_to_operand_aliasing={{}: (10, {})} | custom-call | flops 1358954 | bytes 7077 | tf_op jit(solution)/shard_map/finish/pallas_call | solution.py:332
  (20 shorter events, 0.0 us)
Async XLA Ops:
  0.0 13.1 %copy-start.2 = (s32[8,3]{0,1:T(4,128)S(1)}, s32[8,3]{0,1:T(4,128)}, u32[]{:S(2)}) copy-start(s32[8,3]{0,1:T(4,128)} %param.15) | copy-start | bytes 292
  0.0 11.0 %copy-start.4 = (f32[8,3]{0,1:T(4,128)S(1)}, f32[8,3]{0,1:T(4,128)}, u32[]{:S(2)}) copy-start(f32[8,3]{0,1:T(4,128)} %param.11) | copy-start | bytes 292
  0.0 30.4 %collective-permute-start.5 = (f32[8,384,384]{2,1,0:T(8,128)}, f32[8,384,384]{2,1,0:T(8,128)}, u32[]{:S(2)}, u32[]{:S(2)}) collective-permute-start(f32[8,384,384]{2,1,0:T(8,128)} %own.3), channel_id=1, source_target_pairs={{0,1},{1,0},{2,3},{3,2},{4,5},{5,4},{6,7},{7,6},{8,9},{9,8},{10,11... | collective-permute-start | bytes 14155784 | tf_op jit(solution)/shard_map/ppermute | solution.py:479
  0.8 26.1 %copy-start.1 = (s32[8,3]{1,0:T(8,128)}, s32[8,3]{1,0:T(8,128)S(1)}, u32[]{:S(2)}) copy-start(s32[8,3]{1,0:T(8,128)S(1)} %copy.16.couplings) | copy-start | bytes 292
  0.8 10.1 %collective-permute-start = (s32[8,3]{1,0:T(8,128)S(1)}, s32[8,3]{1,0:T(8,128)S(1)}, u32[]{:S(2)}, u32[]{:S(2)}) collective-permute-start(s32[8,3]{1,0:T(8,128)S(1)} %copy.16.couplings), channel_id=1, source_target_pairs={{0,31},{1,2},{2,1},{3,4},{4,3},{5,6},{6,5},{7,8},{8,7},{9,10},{10,... | collective-permute-start | bytes 296 | tf_op jit(solution)/shard_map/ppermute | solution.py:479
  3.4 64.6 %collective-permute-start.8 = (f32[2,384,768]{2,1,0:T(8,128)}, f32[2,384,768]{2,1,0:T(8,128)}, u32[]{:S(2)}, u32[]{:S(2)}) collective-permute-start(f32[2,384,768]{2,1,0:T(8,128)} %slabs.3), channel_id=1, source_target_pairs={{0,1},{1,0},{2,3},{3,2},{4,5},{5,4},{6,7},{7,6},{8,9},{9,8},{10,11... | collective-permute-start | bytes 7077896 | tf_op jit(solution)/shard_map/ppermute | solution.py:479
  10.9 16.0 %copy-start.3 = (s32[8,3]{1,0:T(8,128)}, s32[8,3]{1,0:T(8,128)S(1)}, u32[]{:S(2)}) copy-start(s32[8,3]{1,0:T(8,128)S(1)} %collective-permute-done.lists_cross) | copy-start | bytes 292
  10.9 19.5 %collective-permute-start.2 = (f32[2,128,768]{2,1,0:T(8,128)}, f32[2,128,768]{2,1,0:T(8,128)}, u32[]{:S(2)}, u32[]{:S(2)}) collective-permute-start(f32[2,128,768]{2,1,0:T(8,128)} %get-tuple-element.34), channel_id=1, source_target_pairs={{0,2},{1,3},{2,0},{3,1},{4,6},{5,7},{6,4},{7,5},{8,10},{9,11},{10,... | collective-permute-start | bytes 2359304 | tf_op jit(solution)/shard_map/ppermute | solution.py:479
  11.6 35.6 %collective-permute-start.4 = (f32[2,128,768]{2,1,0:T(8,128)}, f32[2,128,768]{2,1,0:T(8,128)}, u32[]{:S(2)}, u32[]{:S(2)}) collective-permute-start(f32[2,128,768]{2,1,0:T(8,128)} %get-tuple-element.35), channel_id=1, source_target_pairs={{0,2},{1,3},{2,0},{3,1},{4,6},{5,7},{6,4},{7,5},{8,10},{9,11},{10,... | collective-permute-start | bytes 2359304 | tf_op jit(solution)/shard_map/ppermute | solution.py:479
  13.7 50.4 %collective-permute-start.1 = (f32[2,128,768]{2,1,0:T(8,128)}, f32[2,128,768]{2,1,0:T(8,128)}, u32[]{:S(2)}, u32[]{:S(2)}) collective-permute-start(f32[2,128,768]{2,1,0:T(8,128)} %get-tuple-element.33), channel_id=1, source_target_pairs={{0,2},{1,3},{2,0},{3,1},{4,6},{5,7},{6,4},{7,5},{8,10},{9,11},{10,... | collective-permute-start | bytes 2359304 | tf_op jit(solution)/shard_map/ppermute | solution.py:479
  27.0 20.3 %copy-start.5 = (s32[8,2]{0,1:T(2,128)S(1)}, s32[8,2]{0,1:T(2,128)}, u32[]{:S(2)}) copy-start(s32[8,2]{0,1:T(2,128)} %param.14) | copy-start | bytes 196
  30.4 33.7 %collective-permute-start.3 = (f32[2,128,768]{2,1,0:T(8,128)}, f32[2,128,768]{2,1,0:T(8,128)}, u32[]{:S(2)}, u32[]{:S(2)}) collective-permute-start(f32[2,128,768]{2,1,0:T(8,128)} %collective-permute-done.2.rest_1_), channel_id=1, source_target_pairs={{0,4},{1,5},{2,30},{3,31},{4,8},{5,9},{6,2},{7,3},{8,12},{9,13},{1... | collective-permute-start | bytes 2359304 | tf_op jit(solution)/shard_map/ppermute | solution.py:479
  47.3 33.5 %collective-permute-start.6 = (f32[2,128,768]{2,1,0:T(8,128)}, f32[2,128,768]{2,1,0:T(8,128)}, u32[]{:S(2)}, u32[]{:S(2)}) collective-permute-start(f32[2,128,768]{2,1,0:T(8,128)} %collective-permute-done.4.rest_2_), channel_id=1, source_target_pairs={{0,4},{1,5},{2,30},{3,31},{4,8},{5,9},{6,2},{7,3},{8,12},{9,13},{1... | collective-permute-start | bytes 2359304 | tf_op jit(solution)/shard_map/ppermute | solution.py:479
  64.1 34.1 %collective-permute-start.7 = (f32[2,128,768]{2,1,0:T(8,128)}, f32[2,128,768]{2,1,0:T(8,128)}, u32[]{:S(2)}, u32[]{:S(2)}) collective-permute-start(f32[2,128,768]{2,1,0:T(8,128)} %collective-permute-done.1.rest_3_), channel_id=1, source_target_pairs={{0,4},{1,5},{2,30},{3,31},{4,8},{5,9},{6,2},{7,3},{8,12},{9,13},{1... | collective-permute-start | bytes 2359304 | tf_op jit(solution)/shard_map/ppermute | solution.py:479
  66.3 37.4 %collective-permute-start.9 = (f32[2,128,768]{2,1,0:T(8,128)}, f32[2,128,768]{2,1,0:T(8,128)}, u32[]{:S(2)}, u32[]{:S(2)}) collective-permute-start(f32[2,128,768]{2,1,0:T(8,128)} %broadcast_select_fusion.2), channel_id=1, source_target_pairs={{0,1},{1,0},{2,3},{3,2},{4,5},{5,4},{6,7},{7,6},{8,9},{9,8},{10,11... | collective-permute-start | bytes 2359304 | tf_op jit(solution)/shard_map/ppermute | solution.py:479
  67.0 62.0 %collective-permute-start.12 = (f32[2,384,384]{2,1,0:T(8,128)}, f32[2,384,384]{2,1,0:T(8,128)}, u32[]{:S(2)}, u32[]{:S(2)}) collective-permute-start(f32[2,384,384]{2,1,0:T(8,128)} %get-tuple-element.53), channel_id=1, source_target_pairs={{0,31},{1,2},{2,1},{3,4},{4,3},{5,6},{6,5},{7,8},{8,7},{9,10},{10,... | collective-permute-start | bytes 3538952 | tf_op jit(solution)/shard_map/ppermute | solution.py:479
  68.0 51.5 %collective-permute-start.13 = (f32[2,384,384]{2,1,0:T(8,128)}, f32[2,384,384]{2,1,0:T(8,128)}, u32[]{:S(2)}, u32[]{:S(2)}) collective-permute-start(f32[2,384,384]{2,1,0:T(8,128)} %get-tuple-element.54), channel_id=1, source_target_pairs={{0,31},{1,2},{2,1},{3,4},{4,3},{5,6},{6,5},{7,8},{8,7},{9,10},{10,... | collective-permute-start | bytes 3538952 | tf_op jit(solution)/shard_map/ppermute | solution.py:479
  80.7 22.2 %copy-start = (f32[8,384]{1,0:T(8,128)S(1)}, f32[8,384]{1,0:T(8,128)}, u32[]{:S(2)}) copy-start(f32[8,384]{1,0:T(8,128)} %across.7) | copy-start | bytes 36868
  82.0 21.7 %collective-permute-start.10 = (f32[2,128,768]{2,1,0:T(8,128)S(1)}, f32[2,128,768]{2,1,0:T(8,128)}, u32[]{:S(2)}, u32[]{:S(2)}) collective-permute-start(f32[2,128,768]{2,1,0:T(8,128)S(1)} %broadcast_select_fusion.1), channel_id=1, source_target_pairs={{0,1},{1,0},{2,3},{3,2},{4,5},{5,4},{6,7},{7,6},{8,9},{9,8},{10,11... | collective-permute-start | bytes 2359304 | tf_op jit(solution)/shard_map/ppermute | solution.py:479
  99.4 5.5 %collective-permute-start.11 = (f32[2,128,768]{2,1,0:T(8,128)S(1)}, f32[2,128,768]{2,1,0:T(8,128)}, u32[]{:S(2)}, u32[]{:S(2)}) collective-permute-start(f32[2,128,768]{2,1,0:T(8,128)S(1)} %broadcast_select_fusion), channel_id=1, source_target_pairs={{0,1},{1,0},{2,3},{3,2},{4,5},{5,4},{6,7},{7,6},{8,9},{9,8},{10,11... | collective-permute-start | bytes 2359304 | tf_op jit(solution)/shard_map/ppermute | solution.py:479
  138.2 15.8 %collective-permute-start.14 = (f32[8,384,384]{2,1,0:T(8,128)}, f32[8,384,384]{2,1,0:T(8,128)}, u32[]{:S(2)}, u32[]{:S(2)}) collective-permute-start(f32[8,384,384]{2,1,0:T(8,128)} %get-tuple-element.58.t.own), channel_id=1, source_target_pairs={{0,1},{1,0},{2,3},{3,2},{4,5},{5,4},{6,7},{7,6},{8,9},{9,8},{10,11... | collective-permute-start | bytes 14155784 | tf_op jit(solution)/shard_map/ppermute | solution.py:479
  138.3 47.5 %collective-permute-start.16 = (f32[3,384,384]{2,1,0:T(8,128)}, f32[3,384,384]{2,1,0:T(8,128)}, u32[]{:S(2)}, u32[]{:S(2)}) collective-permute-start(f32[3,384,384]{2,1,0:T(8,128)} %get-tuple-element.60), channel_id=1, source_target_pairs={{0,31},{1,2},{2,1},{3,4},{4,3},{5,6},{6,5},{7,8},{8,7},{9,10},{10,... | collective-permute-start | bytes 5308424 | tf_op jit(solution)/shard_map/ppermute | solution.py:479
  140.8 57.2 %collective-permute-start.15 = (f32[1,384,384]{2,1,0:T(8,128)}, f32[1,384,384]{2,1,0:T(8,128)}, u32[]{:S(2)}, u32[]{:S(2)}) collective-permute-start(f32[1,384,384]{2,1,0:T(8,128)} %get-tuple-element.59), channel_id=1, source_target_pairs={{0,31},{1,2},{2,1},{3,4},{4,3},{5,6},{6,5},{7,8},{8,7},{9,10},{10,... | collective-permute-start | bytes 1769480 | tf_op jit(solution)/shard_map/ppermute | solution.py:479
